TPU v7x, 32 devices: a whole 2x2x4 slice. The times are simulated.
32 devices in a mesh: ctx: 8 (over y, x, core), head: 4 (over z).
Axes of the slice: x: 2, y: 2, z: 4, core: 2. Of those that a mesh axis runs over, the one named last changes fastest.
Arguments:
- queries: bfloat16 [32, 16384, 128], P('head', 'ctx'), may hold values from -6 to 6
- key_states: bfloat16 [16, 16384, 128], P('head', 'ctx'), may hold values from -6 to 6
- value_states: bfloat16 [16, 16384, 128], P('head', 'ctx'), may hold values from -6 to 6
- attn_output: bfloat16 [16384, 4096], P(('ctx', 'head')), may hold values from -6 to 6
- out_cotangent: bfloat16 [16384, 4096], P(('ctx', 'head')), may hold values from -6 to 6
- logsumexp: float32 [32, 16384], P('head', 'ctx'), may hold values from 4.5 to 6.5
- doc_start: int32 [16384], P('ctx'), may hold values from 0 to 15360, as said below
Outputs:
- grad_queries: bfloat16 [32, 16384, 128], P('head', 'ctx')
- grad_keys: bfloat16 [16, 16384, 128], P('head', 'ctx')
- grad_values: bfloat16 [16, 16384, 128], P('head', 'ctx')
Inputs may be any that keep to these rules, and one draw needn't show every extreme that they name: doc_start[t] <= t and never falls; each value is the first position of a document; doc_start[0] = 0; the last 1024 positions form one document that starts at 15360; every other document has half of 1024 to 3072 tokens, except that the one just before the last may be shorter.
All inputs are finite; a program needn't handle non-finite values.
Results may differ from a plain program's by a relative error of at most 0.0049.
Values may be sent and summed in bfloat16 or wider, within the bound.
No kernel may reach another device: no remote copies, remote signals or barrier semaphores. Data moves between devices by JAX's collectives and lax.ppermute only.
A program may use at most 192 MiB of HBM per device.

v0:
```python
import functools
import math

import jax
import jax.numpy as jnp
from jax import lax
from jax.experimental import pallas as pl
from jax.experimental.pallas import tpu as pltpu
from jax.sharding import PartitionSpec as P

W = 1024
QPRE = 168
BLOCK = 128
SUB = 32
UNROLL = 4
VMEM_LIMIT = 60 * 1024 * 1024
LOG2E = math.log2(math.e)
F32 = jnp.float32
BF16 = jnp.bfloat16
NT = (((1,), (1,)), ((), ()))
NN = (((1,), (0,)), ((), ()))


def from_behind(block, axis, distance):
    devices = range(lax.axis_size(axis))
    route = [(i - distance, i) for i in devices if i - distance in devices]
    return lax.ppermute(block, axis, route)


def pack_kernel(pieces, ends, me_ref, *refs):
    cotan_refs, output_refs = refs[:pieces], refs[pieces : 2 * pieces]
    end_refs = refs[2 * pieces : 2 * pieces + ends]
    refs = refs[2 * pieces + ends + 1 :]
    out_refs, rows_ref = refs[:pieces], refs[-1]
    for i in range(ends):
        refs[pieces][i] = end_refs[i][...]
    rows, cols = cotan_refs[0].shape
    groups = cols // BLOCK
    in_piece = rows // BLOCK
    head_of = lax.broadcasted_iota(jnp.int32, (16, cols), 1) // BLOCK
    member = (head_of == lax.broadcasted_iota(jnp.int32, (16, cols), 0)).astype(BF16)
    rows_ref[...] = jnp.zeros_like(rows_ref)
    for k in range(pieces):
        cotan = cotan_refs[k][...]
        product = cotan.astype(F32) * output_refs[k][...].astype(F32)
        high = product.astype(BF16)
        low = (product - high.astype(F32)).astype(BF16)
        delta = lax.dot_general(member, high, NT, preferred_element_type=F32)
        delta = delta + lax.dot_general(member, low, NT, preferred_element_type=F32)
        out_refs[k][:rows] = cotan
        for part in range(3):
            rounded = delta.astype(BF16).astype(F32)
            delta = delta - rounded
            for j in range(in_piece):
                for i in range(groups):
                    rows_ref[
                        part * in_piece + j : part * in_piece + j + 1, i * BLOCK : (i + 1) * BLOCK
                    ] = rounded[i : i + 1, j * BLOCK : (j + 1) * BLOCK]
        out_refs[k][rows:] = rows_ref[...].astype(BF16)


def pack_call(head, me, cotan, output, kv_heads, cols, pieces, after, ends=(), ends_of=0):
    rows = cotan.shape[0]
    assert 3 * (rows // BLOCK) <= 16

    def piece_at(k):
        return pl.BlockSpec(
            (rows, cols), lambda i, me: (0, lax.rem(me[0] + k, pieces) * kv_heads + head)
        )

    in_specs = [piece_at(k) for k in range(pieces)] * 2
    for array in ends:
        last = array.shape[1] // W - 1
        in_specs += [pl.BlockSpec((ends_of, W, array.shape[2]), lambda i, me: (0, last, 0))]
    in_specs += [pl.BlockSpec(memory_space=pl.ANY)]
    operands = [cotan] * pieces + [output] * pieces + [*ends, after]
    out_specs = [pl.BlockSpec((rows + 16, cols), lambda i, me: (0, 0))] * pieces
    out_shape = [jax.ShapeDtypeStruct((rows + 16, cols), BF16)] * pieces
    if ends:
        shape = (len(ends), ends_of, W, ends[0].shape[2])
        out_specs += [pl.BlockSpec(shape, lambda i, me: (0, 0, 0, 0))]
        out_shape += [jax.ShapeDtypeStruct(shape, BF16)]
    scratch = [pltpu.VMEM((16, cols), F32)]
    return pl.pallas_call(
        functools.partial(pack_kernel, pieces, len(ends)),
        grid_spec=pltpu.PrefetchScalarGridSpec(
            num_scalar_prefetch=1,
            grid=(1,),
            in_specs=in_specs,
            out_specs=out_specs,
            scratch_shapes=scratch,
        ),
        out_shape=out_shape,
        compiler_params=pltpu.CompilerParams(vmem_limit_bytes=VMEM_LIMIT),
        cost_estimate=pl.CostEstimate(
            flops=4 * rows * cols * pieces, bytes_accessed=6 * rows * cols * pieces, transcendentals=0
        ),
        name="pack_cotangent",
    )(me, *operands)


def rim_kernel(key_ref, value_ref, after_ref, out_ref):
    out_ref[0] = key_ref[...]
    out_ref[1] = value_ref[...]


def rim_call(keys, values, from_head, after):
    kv_heads, tok_rows, head_dim = keys.shape
    last = pl.BlockSpec((1, W, head_dim), lambda i: (i + from_head, tok_rows // W - 1, 0))
    return pl.pallas_call(
        rim_kernel,
        grid=(kv_heads - from_head,),
        in_specs=[last, last, pl.BlockSpec(memory_space=pl.ANY)],
        out_specs=pl.BlockSpec((2, 1, W, head_dim), lambda i: (0, i, 0, 0)),
        out_shape=jax.ShapeDtypeStruct((2, kv_heads - from_head, W, head_dim), BF16),
        name="rims",
    )(keys, values, after)


def head_kernel(head, window, tok_rows, blocks, carried, aliased, passed, me_ref, *refs):
    q_ref, kh_ref, ko_ref, vh_ref, vo_ref, lse_ref, start_ref = refs[:7]
    groups, _, head_dim = q_ref.shape
    first_block, count = blocks
    opening = first_block == 0
    closing = first_block + count == tok_rows // BLOCK
    outputs = 1 + (4 if closing else 2) + opening
    pieces = len(refs) - 7 - 2 * carried - aliased - 2 * passed - outputs - 8
    cotan_refs = refs[7 : 7 + pieces]
    refs = refs[7 + pieces :]
    carry_refs = refs[: 2 * carried]
    refs = refs[2 * carried + aliased + passed :]
    dq_ref = refs[0]
    k_all, v_all, kt_all, cotan_all, delta_all, ds_all, dk_all, dv_all = refs[outputs + passed :]
    piece_rows = tok_rows // pieces
    in_piece = piece_rows // BLOCK
    span = window + BLOCK
    cols = groups * BLOCK
    scale = QPRE ** (-0.5)
    me = me_ref[0]
    base = first_block * BLOCK
    extent = k_all.shape[0]
    in_rim = max(window - base, 0)

    for all_ref, rim_ref, own_ref in ((k_all, kh_ref, ko_ref), (v_all, vh_ref, vo_ref)):
        if in_rim:
            all_ref[:in_rim] = rim_ref[base:]
        skip = base + in_rim - window
        all_ref[in_rim:] = own_ref[0, skip : skip + extent - in_rim]
    unit = (
        lax.broadcasted_iota(jnp.int32, (head_dim, head_dim), 0)
        == lax.broadcasted_iota(jnp.int32, (head_dim, head_dim), 1)
    ).astype(BF16)
    kt_all[...] = lax.dot_general(unit, k_all[...], NT, preferred_element_type=F32).astype(BF16)
    dk_all[...] = jnp.zeros_like(dk_all)
    dv_all[...] = jnp.zeros_like(dv_all)
    for all_ref, carry_ref in zip((dk_all, dv_all), carry_refs):
        all_ref[: carry_ref.shape[0]] = carry_ref[...]
    ds_all[ds_all.shape[0] - 1] = jnp.zeros(ds_all.shape[1:], BF16)
    for i in range(pieces):
        source = lax.rem(me - i + pieces, pieces)
        where = pl.ds(pl.multiple_of(source * piece_rows, piece_rows), piece_rows)
        for j in range(groups):
            cotan_all[j, where, :] = cotan_refs[i][:piece_rows, j * head_dim : (j + 1) * head_dim]
        parts = cotan_refs[i][piece_rows:].astype(F32)
        for j in range(in_piece):
            row = parts[j : j + 1] + parts[in_piece + j : in_piece + j + 1]
            delta_all[source * in_piece + j] = row + parts[2 * in_piece + j : 2 * in_piece + j + 1]

    def write_query(first, slot):
        dq = lax.dot_general(
            kt_all[:, pl.ds(first, span)], ds_all[slot], NN, preferred_element_type=F32
        )
        dq = (dq.T * F32(scale)).astype(BF16)
        dq_ref[:, pl.ds(first, BLOCK), :] = dq.reshape(groups, BLOCK, head_dim)

    token = lax.broadcasted_iota(jnp.int32, (1, cols), 1) % BLOCK
    place = lax.broadcasted_iota(jnp.int32, (SUB, cols), 0)
    chunks = span // BLOCK
    unroll = ds_all.shape[0]

    def load(index):
        first = pl.multiple_of(index * BLOCK, BLOCK)
        token_first = pl.multiple_of(base + first, BLOCK)
        here = pl.ds(token_first, BLOCK)
        query = q_ref[:, pl.ds(first, BLOCK), :].reshape(cols, head_dim)
        cotan = cotan_all[:, here, :].reshape(cols, head_dim)
        rows = [lse_ref[head * groups + i : head * groups + i + 1, here] for i in range(groups)]
        lse = jnp.concatenate(rows, axis=1) * F32(LOG2E)
        delta = delta_all[first_block + index]
        start = jnp.concatenate([start_ref[:, here]] * groups, axis=1) - token_first
        lower = jnp.maximum(start, token + 1)
        return first, query, cotan, lse, delta, lower

    def span_of(first, i):
        return pl.ds(pl.multiple_of(first + i * BLOCK, BLOCK), BLOCK)

    def front(block, i):
        first, query, cotan = block[:3]
        rows = span_of(first, i)
        return (
            lax.dot_general(k_all[rows, :], query, NT, preferred_element_type=F32),
            lax.dot_general(v_all[rows, :], cotan, NT, preferred_element_type=F32),
        )

    def back(block, i, probs_low, dscores):
        first, query, cotan = block[:3]
        rows = span_of(first, i)
        dv_all[rows, :] += lax.dot_general(probs_low, cotan, NN, preferred_element_type=F32)
        dk_all[rows, :] += lax.dot_general(dscores, query, NN, preferred_element_type=F32)

    def middle(block, slot, i, scores, dprobs):
        _, _, _, lse, delta, lower = block
        lows = []
        for at in range(0, BLOCK, SUB):
            part = slice(at, at + SUB)
            shift = i * BLOCK + at
            allowed = place >= lower - shift
            if shift + SUB > window:
                allowed = allowed & (place <= token + (window - shift))
            probs = jnp.where(
                allowed, jnp.exp2(scores[part] * F32(scale * LOG2E) - lse), F32(0.0)
            )
            dscores = (probs * (dprobs[part] - delta)).astype(BF16)
            ds_all[slot, shift : shift + SUB, :] = dscores
            lows.append((probs.astype(BF16), dscores))
        probs_low = jnp.concatenate([x for x, _ in lows], axis=0)
        dscores = jnp.concatenate([x for _, x in lows], axis=0)
        return probs_low, dscores

    def some_blocks(index, nothing):
        blocks = [load(unroll * index + j) for j in range(unroll)]
        stages = [(j, i) for j in range(unroll) for i in range(chunks)]
        ready = front(blocks[0], 0)
        before = jnp.maximum(unroll * index - 1, 0)
        write_query(pl.multiple_of(before * BLOCK, BLOCK), unroll - 1)
        held = None
        for n, (j, i) in enumerate(stages):
            scores, dprobs = ready
            if n + 1 < len(stages):
                jj, ii = stages[n + 1]
                ready = front(blocks[jj], ii)
            if held is not None:
                back(*held)
            if i == 1 and j > 0:
                write_query(blocks[j - 1][0], j - 1)
            held = (blocks[j], i, *middle(blocks[j], j, i, scores, dprobs))
        back(*held)
        return nothing

    lax.fori_loop(0, count // unroll, some_blocks, 0)
    write_query((count - 1) * BLOCK, unroll - 1)

    if closing:
        dk_ref, dv_ref, dk_tail_ref, dv_tail_ref = refs[1:5]
        tail = extent - window
        own = tail - dk_ref.shape[1]
        dk_ref[0] = (dk_all[own:tail] * F32(scale)).astype(BF16)
        dv_ref[0] = dv_all[own:tail].astype(BF16)
        dk_tail_ref[0] = (dk_all[tail:] * F32(scale)).astype(BF16)
        dv_tail_ref[0] = dv_all[tail:].astype(BF16)
    else:
        dk_next_ref, dv_next_ref = refs[1:3]
        dk_next_ref[...] = dk_all[extent - window :]
        dv_next_ref[...] = dv_all[extent - window :]
    if opening:
        halo_ref = refs[outputs - 1]
        halo_ref[0, 0] = (dk_all[:window] * F32(scale)).astype(BF16)
        halo_ref[0, 1] = dv_all[:window].astype(BF16)


def head_call(
    head, blocks, me, queries, rims, rim_head, keys, values, lse, start, cotans, before, carry, passing, halo=None
):
    kv_heads, tok_rows, head_dim = keys.shape
    q_heads = queries.shape[0]
    groups = q_heads // kv_heads
    window = rims.shape[2]
    pieces = len(cotans)
    own = tok_rows - window
    first_block, count = blocks
    assert first_block % count == 0
    extent = count * BLOCK + window
    rim_rows = window if first_block == 0 else BLOCK
    own_rows = min(first_block * BLOCK + extent - window, tok_rows)

    def at_head(*block):
        return pl.BlockSpec(block, lambda i, me: (head, 0, 0))

    def full(*block):
        return pl.BlockSpec(block, lambda i, me: (0,) * len(block))

    q_spec = pl.BlockSpec(
        (groups, count * BLOCK, head_dim), lambda i, me: (head, first_block // count, 0)
    )
    in_specs = [
        q_spec,
        pl.BlockSpec((None, None, rim_rows, head_dim), lambda i, me: (0, rim_head, 0, 0)),
        at_head(1, own_rows, head_dim),
        pl.BlockSpec((None, None, rim_rows, head_dim), lambda i, me: (1, rim_head, 0, 0)),
        at_head(1, own_rows, head_dim),
        full(q_heads, tok_rows),
        full(1, tok_rows),
    ]
    in_specs += [full(*cotans[0].shape)] * pieces
    in_specs += [full(*array.shape) for array in carry]
    n_in = 1 + 7 + pieces + len(carry)
    aliases = {n_in + i: i for i in range(len(before))}
    unroll = math.gcd(UNROLL, count)
    out_specs = [q_spec]
    out_shape = [jax.ShapeDtypeStruct(queries.shape, BF16)]
    if first_block + count == tok_rows // BLOCK:
        out_specs += [at_head(1, own, head_dim)] * 2 + [at_head(1, window, head_dim)] * 2
        out_shape += [jax.ShapeDtypeStruct(keys.shape, BF16)] * 2
        out_shape += [jax.ShapeDtypeStruct((kv_heads, window, head_dim), BF16)] * 2
    else:
        out_specs += [full(window, head_dim)] * 2
        out_shape += [jax.ShapeDtypeStruct((window, head_dim), F32)] * 2
    if first_block == 0:
        slot, size, earlier = halo
        out_specs += [pl.BlockSpec((1, 2, window, head_dim), lambda i, me: (slot, 0, 0, 0))]
        out_shape += [jax.ShapeDtypeStruct((size, 2, window, head_dim), BF16)]
        if earlier is not None:
            aliases[n_in + len(before)] = len(out_shape) - 1
            before = [*before, earlier]
    scratch = [
        pltpu.VMEM((extent, head_dim), BF16),
        pltpu.VMEM((extent, head_dim), BF16),
        pltpu.VMEM((head_dim, extent), BF16),
        pltpu.VMEM((groups, tok_rows, head_dim), BF16),
        pltpu.VMEM((tok_rows // BLOCK, 1, groups * BLOCK), F32),
        pltpu.VMEM((unroll, window + BLOCK, groups * BLOCK), BF16),
        pltpu.VMEM((extent, head_dim), F32),
        pltpu.VMEM((extent, head_dim), F32),
    ]
    in_specs += [pl.BlockSpec(memory_space=pl.ANY)] * (len(before) + len(passing))
    for i, array in enumerate(passing):
        aliases[n_in + len(before) + i] = len(out_shape)
        out_shape.append(jax.ShapeDtypeStruct(array.shape, array.dtype))
        out_specs.append(pl.BlockSpec(memory_space=pl.ANY))
    pairs = groups * count * BLOCK * (window + BLOCK)
    return pl.pallas_call(
        functools.partial(
            head_kernel, head, window, tok_rows, blocks, len(carry) // 2, len(before), len(passing)
        ),
        grid_spec=pltpu.PrefetchScalarGridSpec(
            num_scalar_prefetch=1,
            grid=(1,),
            in_specs=in_specs,
            out_specs=out_specs,
            scratch_shapes=scratch,
        ),
        out_shape=out_shape,
        input_output_aliases=aliases,
        compiler_params=pltpu.CompilerParams(vmem_limit_bytes=VMEM_LIMIT),
        cost_estimate=pl.CostEstimate(
            flops=40 * pairs * head_dim, bytes_accessed=8 * tok_rows, transcendentals=0
        ),
        name="head_backward",
    )(me, queries, rims, keys, rims, values, lse, start, *cotans, *carry, *before, *passing)


def join_kernel(joint, dk_tail_ref, dv_tail_ref, *refs):
    backs = refs[:-4]
    dk_ref, dv_ref = refs[-2:]

    def join(back_ref):
        dk_ref[...] = (dk_tail_ref[...].astype(F32) + back_ref[:, 0].astype(F32)).astype(BF16)
        dv_ref[...] = (dv_tail_ref[...].astype(F32) + back_ref[:, 1].astype(F32)).astype(BF16)

    if len(backs) == 1:
        join(backs[0])
    else:
        pl.when(pl.program_id(0) < joint)(lambda: join(backs[0]))
        pl.when(pl.program_id(0) >= joint)(lambda: join(backs[1]))


def join_call(dk_tail, dv_tail, backs, grad_keys, grad_values):
    kv_heads, window, head_dim = dk_tail.shape
    last = grad_keys.shape[1] // window - 1
    joint = backs[0].shape[0]
    tail = pl.BlockSpec((1, window, head_dim), lambda i: (i, 0, 0))
    out = pl.BlockSpec((1, window, head_dim), lambda i: (i, last, 0))
    anywhere = pl.BlockSpec(memory_space=pl.ANY)
    shape = (1, 2, window, head_dim)
    back_specs = [pl.BlockSpec(shape, lambda i: (jnp.minimum(i, joint - 1), 0, 0, 0))]
    back_specs += [pl.BlockSpec(shape, lambda i: (0, 0, 0, 0))] * (len(backs) - 1)
    return pl.pallas_call(
        functools.partial(join_kernel, joint),
        grid=(kv_heads,),
        in_specs=[tail, tail, *back_specs, anywhere, anywhere],
        out_specs=[out, out],
        out_shape=[jax.ShapeDtypeStruct(grad_keys.shape, BF16)] * 2,
        input_output_aliases={2 + len(backs): 0, 3 + len(backs): 1},
        compiler_params=pltpu.CompilerParams(vmem_limit_bytes=VMEM_LIMIT),
        name="join_tails",
    )(dk_tail, dv_tail, *backs, grad_keys, grad_values)


def body(queries, key_states, value_states, attn_output, out_cotangent, logsumexp, doc_start):
    kv_heads, tok_rows, head_dim = key_states.shape
    groups = queries.shape[0] // kv_heads
    pieces = lax.axis_size("head")
    me = lax.axis_index("head").astype(jnp.int32)[None]
    start = doc_start[None, :] - lax.axis_index("ctx") * tok_rows + W
    steps = tok_rows // BLOCK

    def sent(block, distance):
        route = [(i, (i + distance) % pieces) for i in range(pieces)]
        return lax.ppermute(block, "head", route)

    def packed(head, after, *ends):
        return pack_call(
            head, me, out_cotangent, attn_output, kv_heads, groups * head_dim, pieces, after, *ends
        )

    def arrived(parts):
        return [part if k == 0 else sent(part, k) for k, part in enumerate(parts)]

    early = (kv_heads + 1) // 2
    *first, ends = packed(0, out_cotangent, (key_states, value_states), early)
    parts = {0: first}
    cotans = {0: arrived(first)}
    rims = [from_behind(ends, "ctx", 1)]
    after = first[0]
    for head in range(kv_heads - 1, 0, -1):
        parts[head] = packed(head, after)
        after = parts[head][0]
    if kv_heads > 1:
        held = lax.optimization_barrier((*parts[1], *cotans[0][1:]))
        parts[1], cotans[0][1:] = list(held[:pieces]), held[pieces:]
        cotans[1] = arrived(parts[1])
    if kv_heads > early:
        ends = rim_call(key_states, value_states, early, after)
        rims.append(from_behind(ends, "ctx", 1))

    split = 2 * W == tok_rows
    final = kv_heads - 1 if split else kv_heads
    before = []
    halos = None
    backs = []
    for head in range(kv_heads):
        later = parts[head + 2] if head + 2 < kv_heads else []
        halo = (head, final, halos) if head < final else (0, 1, None)
        call = functools.partial(
            head_call, head, me=me, queries=queries, rims=rims[int(head >= early)],
            rim_head=head - early * (head >= early), keys=key_states, values=value_states,
            lse=logsumexp, start=start, cotans=cotans[head], halo=halo,
        )
        if head + 1 < kv_heads or not split:
            got = call((0, steps), before=before, carry=[], passing=later[1:])
            if later:
                middle = pieces // 2
                moving = list(got[6:])
                held = lax.optimization_barrier((moving[middle - 1], *cotans[head + 1][1:]))
                moving[middle - 1] = held[0]
                cotans[head + 1][1:] = held[1:]
                cotans[head + 2] = arrived([later[0], *moving])
            before, halos = list(got[:5]), got[5]
        else:
            got = call((0, steps // 2), before=before[:1], carry=[], passing=[])
            halos = got[3]
        if head >= final - 1:
            backs.append(from_behind(halos, "ctx", -1))
        if head + 1 == kv_heads and split:
            before = call(
                (steps // 2, steps // 2), before=[got[0], *before[1:]], carry=got[1:3], passing=[]
            )
    grad_queries, grad_keys, grad_values, *tails = before
    grad_keys, grad_values = join_call(*tails, backs, grad_keys, grad_values)
    return grad_queries, grad_keys, grad_values


def solution(mesh):
    return jax.shard_map(
        body,
        mesh=mesh,
        in_specs=(
            P("head", "ctx", None),
            P("head", "ctx", None),
            P("head", "ctx", None),
            P(("ctx", "head"), None),
            P(("ctx", "head"), None),
            P("head", "ctx"),
            P("ctx"),
        ),
        out_specs=(P("head", "ctx", None), P("head", "ctx", None), P("head", "ctx", None)),
        check_vma=False,
    )
```

profile of v0, /device:TPU:1, one launch (start us, length us, event | category | flops | bytes accessed | tf_op | source)
XLA Modules:
  0.0 140.1 jit_solution(4224879329303542526)
XLA Ops:
  0.6 3.7 %pack_cotangent.4 = (bf16[528,256]{1,0:T(8,128)(2,1)}, bf16[528,256]{1,0:T(8,128)(2,1)}, bf16[528,256]{1,0:T(8,128)(2,1)}, bf16[528,256]{1,0:T(8,128)(2,1)}, bf16[2,2,1024,128]{3,2,1,0:T(8,128)(2,1)}) custom-call(s32[1]{0:T(128)} %bitcast.me_ref, bf16[512,4096]{1,0:T(8,128)(2,1)} %refs_3_.7, bf16[512,4096]{1,0:T(8,128)(2,1)} %refs_3_.7, ...), custom_call_target="tpu_custom_call" | custom-call | flops 2097152 | bytes 3145728 | tf_op jit(solution)/shard_map/pack_cotangent/pallas_call | solution.py:84
  4.3 4.5 %collective-permute-start.1 = (bf16[2,2,1024,128]{3,2,1,0:T(8,128)(2,1)}, bf16[2,2,1024,128]{3,2,1,0:T(8,128)(2,1)S(1)}, u32[]{:S(2)}, u32[]{:S(2)}) collective-permute-start(bf16[2,2,1024,128]{3,2,1,0:T(8,128)(2,1)} %get-tuple-element.74), channel_id=1, source_target_pairs={{0,4},{4,8},{8,12},{12,16},{16,20},{20,24},{24,28},{1,5},{5,9},{9,... | collective-permute-start | bytes 3145736 | tf_op jit(solution)/shard_map/ppermute | solution.py:27
  8.8 1.3 collective-permute-start.2
  10.2 2.3 %collective-permute-start.3 = (bf16[528,256]{1,0:T(8,128)(2,1)}, bf16[528,256]{1,0:T(8,128)(2,1)S(1)}, u32[]{:S(2)}, u32[]{:S(2)}) collective-permute-start(bf16[528,256]{1,0:T(8,128)(2,1)} %get-tuple-element.79), channel_id=1, source_target_pairs={{0,2},{1,3},{2,0},{3,1},{4,6},{5,7},{6,4},{7,5},{8,10},{9,11},{10,... | collective-permute-start | bytes 811016 | tf_op jit(solution)/shard_map/ppermute | solution.py:409
  13.6 3.0 %pack_cotangent.5 = (bf16[528,256]{1,0:T(8,128)(2,1)}, bf16[528,256]{1,0:T(8,128)(2,1)}, bf16[528,256]{1,0:T(8,128)(2,1)}, bf16[528,256]{1,0:T(8,128)(2,1)}) custom-call(s32[1]{0:T(128)} %bitcast.me_ref, bf16[512,4096]{1,0:T(8,128)(2,1)} %refs_3_.7, bf16[512,4096]{1,0:T(8,128)(2,1)} %refs_3_.7, bf16[512,4096]{1,0:T(8,128)(2,1)} %refs_3_.7, ...), custom_call_target="tpu_custom_call" | custom-call | flops 2097152 | bytes 3145728 | tf_op jit(solution)/shard_map/pack_cotangent/pallas_call | solution.py:84
  16.5 3.0 %pack_cotangent.6 = (bf16[528,256]{1,0:T(8,128)(2,1)}, bf16[528,256]{1,0:T(8,128)(2,1)}, bf16[528,256]{1,0:T(8,128)(2,1)}, bf16[528,256]{1,0:T(8,128)(2,1)}) custom-call(s32[1]{0:T(128)} %bitcast.me_ref, bf16[512,4096]{1,0:T(8,128)(2,1)} %refs_3_.7, bf16[512,4096]{1,0:T(8,128)(2,1)} %refs_3_.7, bf16[512,4096]{1,0:T(8,128)(2,1)} %refs_3_.7, ...), custom_call_target="tpu_custom_call" | custom-call | flops 2097152 | bytes 3145728 | tf_op jit(solution)/shard_map/pack_cotangent/pallas_call | solution.py:84
  19.5 3.0 %pack_cotangent.7 = (bf16[528,256]{1,0:T(8,128)(2,1)}, bf16[528,256]{1,0:T(8,128)(2,1)}, bf16[528,256]{1,0:T(8,128)(2,1)}, bf16[528,256]{1,0:T(8,128)(2,1)}) custom-call(s32[1]{0:T(128)} %bitcast.me_ref, bf16[512,4096]{1,0:T(8,128)(2,1)} %refs_3_.7, bf16[512,4096]{1,0:T(8,128)(2,1)} %refs_3_.7, bf16[512,4096]{1,0:T(8,128)(2,1)} %refs_3_.7, ...), custom_call_target="tpu_custom_call" | custom-call | flops 2097152 | bytes 3145728 | tf_op jit(solution)/shard_map/pack_cotangent/pallas_call | solution.py:84
  22.5 2.1 %rims.1 = bf16[2,2,1024,128]{3,2,1,0:T(8,128)(2,1)} custom-call(bf16[4,2048,128]{2,1,0:T(8,128)(2,1)} %refs_2_.17, bf16[4,2048,128]{2,1,0:T(8,128)(2,1)} %refs_4_.17, bf16[528,256]{1,0:T(8,128)(2,1)} %get-tuple-element.81.after_ref.refs_7_), custom_call_target="tpu_custom_call" | custom-call | tf_op jit(solution)/shard_map/rims/pallas_call | solution.py:110
  24.6 2.7 %collective-permute-start = (bf16[2,2,1024,128]{3,2,1,0:T(8,128)(2,1)}, bf16[2,2,1024,128]{3,2,1,0:T(8,128)(2,1)S(1)}, u32[]{:S(2)}, u32[]{:S(2)}) collective-permute-start(bf16[2,2,1024,128]{3,2,1,0:T(8,128)(2,1)} %rims.1), channel_id=1, source_target_pairs={{0,4},{4,8},{8,12},{12,16},{16,20},{20,24},{24,28},{1,5},{5,9},{9,... | collective-permute-start | bytes 3145736 | tf_op jit(solution)/shard_map/ppermute | solution.py:27
  28.0 2.0 %collective-permute-done.3.refs_9_ = bf16[528,256]{1,0:T(8,128)(2,1)S(1)} collective-permute-done((bf16[528,256]{1,0:T(8,128)(2,1)}, bf16[528,256]{1,0:T(8,128)(2,1)S(1)}, u32[]{:S(2)}, u32[]{:S(2)}) %collective-permute-start.3) | collective-permute-done | bytes 270368 | tf_op jit(solution)/shard_map/ppermute | solution.py:409
  30.0 6.1 %collective-permute-start.5 = (bf16[528,256]{1,0:T(8,128)(2,1)}, bf16[528,256]{1,0:T(8,128)(2,1)S(1)}, u32[]{:S(2)}, u32[]{:S(2)}) collective-permute-start(bf16[528,256]{1,0:T(8,128)(2,1)} %get-tuple-element.89), channel_id=1, source_target_pairs={{0,1},{1,2},{2,3},{3,0},{4,5},{5,6},{6,7},{7,4},{8,9},{9,10},{10,1... | collective-permute-start | bytes 811016 | tf_op jit(solution)/shard_map/ppermute | solution.py:409
  36.1 1.4 collective-permute-start.6
  39.3 17.4 %head_backward.5 = (bf16[8,2048,128]{2,1,0:T(8,128)(2,1)}, bf16[4,2048,128]{2,1,0:T(8,128)(2,1)}, bf16[4,2048,128]{2,1,0:T(8,128)(2,1)}, bf16[4,1024,128]{2,1,0:...) custom-call(s32[1]{0:T(128)} %bitcast.me_ref, ...), custom_call_target="tpu_custom_call", output_to_operand_aliasing={{6}: (12, {}), {7}: (13, {}), {8}: (14, {})} | custom-call | flops 24159191040 | bytes 16384 | tf_op jit(solution)/shard_map/head_backward/pallas_call | solution.py:341
  57.4 3.6 %collective-permute-start.10 = (bf16[528,256]{1,0:T(8,128)(2,1)}, bf16[528,256]{1,0:T(8,128)(2,1)S(1)}, u32[]{:S(2)}, u32[]{:S(2)}) collective-permute-start(bf16[528,256]{1,0:T(8,128)(2,1)} %get-tuple-element.107), channel_id=1, source_target_pairs={{0,2},{1,3},{2,0},{3,1},{4,6},{5,7},{6,4},{7,5},{8,10},{9,11},{10,... | collective-permute-start | bytes 811016 | tf_op jit(solution)/shard_map/ppermute | solution.py:409
  61.0 3.2 %collective-permute-start.11 = (bf16[528,256]{1,0:T(8,128)(2,1)}, bf16[528,256]{1,0:T(8,128)(2,1)S(1)}, u32[]{:S(2)}, u32[]{:S(2)}) collective-permute-start(bf16[528,256]{1,0:T(8,128)(2,1)} %get-tuple-element.108), channel_id=1, source_target_pairs={{0,3},{1,0},{2,1},{3,2},{4,7},{5,4},{6,5},{7,6},{8,11},{9,8},{10,9... | collective-permute-start | bytes 811016 | tf_op jit(solution)/shard_map/ppermute | solution.py:409
  64.3 17.4 %head_backward.6 = (bf16[8,2048,128]{2,1,0:T(8,128)(2,1)}, bf16[4,2048,128]{2,1,0:T(8,128)(2,1)}, bf16[4,2048,128]{2,1,0:T(8,128)(2,1)}, bf16[4,1024,128]{2,1,0:...) custom-call(s32[1]{0:T(128)} %bitcast.me_ref, ...), custom_call_target="tpu_custom_call", output_to_operand_aliasing={{0}: (12, {}), {1}: (13, {}), {2}: (14, {}), {3}: (15, {}),... | custom-call | flops 24159191040 | bytes 16384 | tf_op jit(solution)/shard_map/head_backward/pallas_call | solution.py:341
  81.6 3.3 %collective-permute-start.13 = (bf16[528,256]{1,0:T(8,128)(2,1)}, bf16[528,256]{1,0:T(8,128)(2,1)S(1)}, u32[]{:S(2)}, u32[]{:S(2)}) collective-permute-start(bf16[528,256]{1,0:T(8,128)(2,1)} %get-tuple-element.110), channel_id=1, source_target_pairs={{0,3},{1,0},{2,1},{3,2},{4,7},{5,4},{6,5},{7,6},{8,11},{9,8},{10,9... | collective-permute-start | bytes 811016 | tf_op jit(solution)/shard_map/ppermute | solution.py:409
  84.9 3.0 %collective-permute-start.12 = (bf16[528,256]{1,0:T(8,128)(2,1)}, bf16[528,256]{1,0:T(8,128)(2,1)S(1)}, u32[]{:S(2)}, u32[]{:S(2)}) collective-permute-start(bf16[528,256]{1,0:T(8,128)(2,1)} %get-tuple-element.109), channel_id=1, source_target_pairs={{0,2},{1,3},{2,0},{3,1},{4,6},{5,7},{6,4},{7,5},{8,10},{9,11},{10,... | collective-permute-start | bytes 811016 | tf_op jit(solution)/shard_map/ppermute | solution.py:409
  89.0 17.4 %head_backward.7 = (bf16[8,2048,128]{2,1,0:T(8,128)(2,1)}, bf16[4,2048,128]{2,1,0:T(8,128)(2,1)}, bf16[4,2048,128]{2,1,0:T(8,128)(2,1)}, bf16[4,1024,128]{2,1,0:...) custom-call(s32[1]{0:T(128)} %bitcast.me_ref, ...), custom_call_target="tpu_custom_call", output_to_operand_aliasing={{0}: (12, {}), {1}: (13, {}), {2}: (14, {}), {3}: (15, {}),... | custom-call | flops 24159191040 | bytes 16384 | tf_op jit(solution)/shard_map/head_backward/pallas_call | solution.py:341
  106.4 3.0 %collective-permute-start.14 = (bf16[3,2,1024,128]{3,2,1,0:T(8,128)(2,1)}, bf16[3,2,1024,128]{3,2,1,0:T(8,128)(2,1)S(1)}, u32[]{:S(2)}, u32[]{:S(2)}) collective-permute-start(bf16[3,2,1024,128]{3,2,1,0:T(8,128)(2,1)} %get-tuple-element.131), channel_id=1, source_target_pairs={{4,0},{8,4},{12,8},{16,12},{20,16},{24,20},{28,24},{5,1},{9,5},{13... | collective-permute-start | bytes 4718600 | tf_op jit(solution)/shard_map/ppermute | solution.py:27
  110.3 10.5 %head_backward.8 = (bf16[8,2048,128]{2,1,0:T(8,128)(2,1)}, f32[1024,128]{1,0:T(8,128)}, f32[1024,128]{1,0:T(8,128)}, bf16[1,2,1024,128]{3,2,1,0:T(8,128)(2,1)}) custom-call(s32[1]{0:T(128)} %bitcast.me_ref, bf16[8,2048,128]{2,1,0:T(8,128)(2,1)} %refs_0_.17, bf16[2,2,1024,128]{3,2,1,0:T(8,128)(2,1)} %copy-done.3, ...), custom_call_target="tpu_custom_call", output_to_operand_aliasing={{0}: (12, {})} | custom-call | flops 12079595520 | bytes 16384 | tf_op jit(solution)/shard_map/head_backward/pallas_call | solution.py:341
  120.8 1.9 %collective-permute-start.15 = (bf16[1,2,1024,128]{3,2,1,0:T(8,128)(2,1)}, bf16[1,2,1024,128]{3,2,1,0:T(8,128)(2,1)S(1)}, u32[]{:S(2)}, u32[]{:S(2)}) collective-permute-start(bf16[1,2,1024,128]{3,2,1,0:T(8,128)(2,1)} %get-tuple-element.132), channel_id=1, source_target_pairs={{4,0},{8,4},{12,8},{16,12},{20,16},{24,20},{28,24},{5,1},{9,5},{13... | collective-permute-start | bytes 1572872 | tf_op jit(solution)/shard_map/ppermute | solution.py:27
  122.7 10.7 %head_backward.9 = (bf16[8,2048,128]{2,1,0:T(8,128)(2,1)}, bf16[4,2048,128]{2,1,0:T(8,128)(2,1)}, bf16[4,2048,128]{2,1,0:T(8,128)(2,1)}, bf16[4,1024,128]{2,1,0:T(8,128)(2,1)}, bf16[4,1024,128]{2,1,0:T(8,128)(2,1)}) custom-call(s32[1]{0:T(128)} %bitcast.me_ref, ...), custom_call_target="tpu_custom_call", output_to_operand_aliasing={{0}: (14, {}), {1}: (15, {}), {2}: (16, {}), {3}: (17, {}),... | custom-call | flops 12079595520 | bytes 16384 | tf_op jit(solution)/shard_map/head_backward/pallas_call | solution.py:341
  135.6 4.4 %join_tails.1 = (bf16[4,2048,128]{2,1,0:T(8,128)(2,1)}, bf16[4,2048,128]{2,1,0:T(8,128)(2,1)}) custom-call(bf16[4,1024,128]{2,1,0:T(8,128)(2,1)} %get-tuple-element.129.dk_tail_ref, bf16[4,1024,128]{2,1,0:T(8,128)(2,1)} %get-tuple-element.130.dv_tail_ref, bf16[3,2,1024,128]{3,2,1,0:T(8,128)(2,1)} %copy-done, ...), custom_call_target="tpu_custom_call", output_to_operand_aliasing={{0}: (4, {}), {1}: (5, {})} | custom-call | tf_op jit(solution)/shard_map/join_tails/pallas_call | solution.py:387
  (56 shorter events, 8.4 us)
Async XLA Ops:
  4.3 33.9 %collective-permute-start.1 = (bf16[2,2,1024,128]{3,2,1,0:T(8,128)(2,1)}, bf16[2,2,1024,128]{3,2,1,0:T(8,128)(2,1)S(1)}, u32[]{:S(2)}, u32[]{:S(2)}) collective-permute-start(bf16[2,2,1024,128]{3,2,1,0:T(8,128)(2,1)} %get-tuple-element.74), channel_id=1, source_target_pairs={{0,4},{4,8},{8,12},{12,16},{16,20},{20,24},{24,28},{1,5},{5,9},{9,... | collective-permute-start | bytes 3145736 | tf_op jit(solution)/shard_map/ppermute | solution.py:27
  8.8 19.2 %collective-permute-start.2 = (bf16[528,256]{1,0:T(8,128)(2,1)}, bf16[528,256]{1,0:T(8,128)(2,1)S(1)}, u32[]{:S(2)}, u32[]{:S(2)}) collective-permute-start(bf16[528,256]{1,0:T(8,128)(2,1)} %get-tuple-element.78), channel_id=1, source_target_pairs={{0,1},{1,2},{2,3},{3,0},{4,5},{5,6},{6,7},{7,4},{8,9},{9,10},{10,1... | collective-permute-start | bytes 811016 | tf_op jit(solution)/shard_map/ppermute | solution.py:409
  10.2 19.8 %collective-permute-start.3 = (bf16[528,256]{1,0:T(8,128)(2,1)}, bf16[528,256]{1,0:T(8,128)(2,1)S(1)}, u32[]{:S(2)}, u32[]{:S(2)}) collective-permute-start(bf16[528,256]{1,0:T(8,128)(2,1)} %get-tuple-element.79), channel_id=1, source_target_pairs={{0,2},{1,3},{2,0},{3,1},{4,6},{5,7},{6,4},{7,5},{8,10},{9,11},{10,... | collective-permute-start | bytes 811016 | tf_op jit(solution)/shard_map/ppermute | solution.py:409
  12.5 17.5 %collective-permute-start.4 = (bf16[528,256]{1,0:T(8,128)(2,1)}, bf16[528,256]{1,0:T(8,128)(2,1)S(1)}, u32[]{:S(2)}, u32[]{:S(2)}) collective-permute-start(bf16[528,256]{1,0:T(8,128)(2,1)} %get-tuple-element.80), channel_id=1, source_target_pairs={{0,3},{1,0},{2,1},{3,2},{4,7},{5,4},{6,5},{7,6},{8,11},{9,8},{10,9... | collective-permute-start | bytes 811016 | tf_op jit(solution)/shard_map/ppermute | solution.py:409
  22.5 4.9 %copy-start.2 = (s32[2048]{0:T(1024)S(1)}, s32[2048]{0:T(1024)}, u32[]{:S(2)}) copy-start(s32[2048]{0:T(1024)} %param.13) | copy-start | bytes 24580
  22.5 13.6 %copy-start.11 = (bf16[528,256]{1,0:T(8,128)(2,1)S(1)}, bf16[528,256]{1,0:T(8,128)(2,1)}, u32[]{:S(2)}) copy-start(bf16[528,256]{1,0:T(8,128)(2,1)} %get-tuple-element.90) | copy-start | bytes 811012
  22.5 15.0 %copy-start.9 = (bf16[528,256]{1,0:T(8,128)(2,1)S(1)}, bf16[528,256]{1,0:T(8,128)(2,1)}, u32[]{:S(2)}) copy-start(bf16[528,256]{1,0:T(8,128)(2,1)} %get-tuple-element.91) | copy-start | bytes 811012
  24.6 63.4 %collective-permute-start = (bf16[2,2,1024,128]{3,2,1,0:T(8,128)(2,1)}, bf16[2,2,1024,128]{3,2,1,0:T(8,128)(2,1)S(1)}, u32[]{:S(2)}, u32[]{:S(2)}) collective-permute-start(bf16[2,2,1024,128]{3,2,1,0:T(8,128)(2,1)} %rims.1), channel_id=1, source_target_pairs={{0,4},{4,8},{8,12},{12,16},{16,20},{20,24},{24,28},{1,5},{5,9},{9,... | collective-permute-start | bytes 3145736 | tf_op jit(solution)/shard_map/ppermute | solution.py:27
  28.0 10.3 %copy-start.5 = (bf16[528,256]{1,0:T(8,128)(2,1)}, bf16[528,256]{1,0:T(8,128)(2,1)S(1)}, u32[]{:S(2)}) copy-start(bf16[528,256]{1,0:T(8,128)(2,1)S(1)} %collective-permute-done.2.refs_8_) | copy-start | bytes 811012
  30.0 8.2 %copy-start.6 = (bf16[528,256]{1,0:T(8,128)(2,1)}, bf16[528,256]{1,0:T(8,128)(2,1)S(1)}, u32[]{:S(2)}) copy-start(bf16[528,256]{1,0:T(8,128)(2,1)S(1)} %collective-permute-done.3.refs_9_) | copy-start | bytes 811012
  30.0 8.2 %copy-start.8 = (bf16[528,256]{1,0:T(8,128)(2,1)}, bf16[528,256]{1,0:T(8,128)(2,1)S(1)}, u32[]{:S(2)}) copy-start(bf16[528,256]{1,0:T(8,128)(2,1)S(1)} %collective-permute-done.4.refs_10_) | copy-start | bytes 811012
  30.0 26.7 %collective-permute-start.5 = (bf16[528,256]{1,0:T(8,128)(2,1)}, bf16[528,256]{1,0:T(8,128)(2,1)S(1)}, u32[]{:S(2)}, u32[]{:S(2)}) collective-permute-start(bf16[528,256]{1,0:T(8,128)(2,1)} %get-tuple-element.89), channel_id=1, source_target_pairs={{0,1},{1,2},{2,3},{3,0},{4,5},{5,6},{6,7},{7,4},{8,9},{9,10},{10,1... | collective-permute-start | bytes 811016 | tf_op jit(solution)/shard_map/ppermute | solution.py:409
  36.1 20.6 %collective-permute-start.6 = (bf16[528,256]{1,0:T(8,128)(2,1)S(1)}, bf16[528,256]{1,0:T(8,128)(2,1)S(1)}, u32[]{:S(2)}, u32[]{:S(2)}) collective-permute-start(bf16[528,256]{1,0:T(8,128)(2,1)S(1)} %copy-done.11), channel_id=1, source_target_pairs={{0,2},{1,3},{2,0},{3,1},{4,6},{5,7},{6,4},{7,5},{8,10},{9,11},{10,... | collective-permute-start | bytes 811016 | tf_op jit(solution)/shard_map/ppermute | solution.py:409
  37.5 19.2 %collective-permute-start.7 = (bf16[528,256]{1,0:T(8,128)(2,1)S(1)}, bf16[528,256]{1,0:T(8,128)(2,1)}, u32[]{:S(2)}, u32[]{:S(2)}) collective-permute-start(bf16[528,256]{1,0:T(8,128)(2,1)S(1)} %copy-done.9), channel_id=1, source_target_pairs={{0,3},{1,0},{2,1},{3,2},{4,7},{5,4},{6,5},{7,6},{8,11},{9,8},{10,9... | collective-permute-start | bytes 811016 | tf_op jit(solution)/shard_map/ppermute | solution.py:409
  56.7 7.6 %copy-start.12 = (bf16[528,256]{1,0:T(8,128)(2,1)}, bf16[528,256]{1,0:T(8,128)(2,1)S(1)}, u32[]{:S(2)}) copy-start(bf16[528,256]{1,0:T(8,128)(2,1)S(1)} %collective-permute-done.5.refs_8_) | copy-start | bytes 811012
  57.4 27.5 %collective-permute-start.10 = (bf16[528,256]{1,0:T(8,128)(2,1)}, bf16[528,256]{1,0:T(8,128)(2,1)S(1)}, u32[]{:S(2)}, u32[]{:S(2)}) collective-permute-start(bf16[528,256]{1,0:T(8,128)(2,1)} %get-tuple-element.107), channel_id=1, source_target_pairs={{0,2},{1,3},{2,0},{3,1},{4,6},{5,7},{6,4},{7,5},{8,10},{9,11},{10,... | collective-permute-start | bytes 811016 | tf_op jit(solution)/shard_map/ppermute | solution.py:409
  61.0 23.9 %collective-permute-start.11 = (bf16[528,256]{1,0:T(8,128)(2,1)}, bf16[528,256]{1,0:T(8,128)(2,1)S(1)}, u32[]{:S(2)}, u32[]{:S(2)}) collective-permute-start(bf16[528,256]{1,0:T(8,128)(2,1)} %get-tuple-element.108), channel_id=1, source_target_pairs={{0,3},{1,0},{2,1},{3,2},{4,7},{5,4},{6,5},{7,6},{8,11},{9,8},{10,9... | collective-permute-start | bytes 811016 | tf_op jit(solution)/shard_map/ppermute | solution.py:409
  64.2 20.7 %collective-permute-start.9 = (bf16[528,256]{1,0:T(8,128)(2,1)}, bf16[528,256]{1,0:T(8,128)(2,1)S(1)}, u32[]{:S(2)}, u32[]{:S(2)}) collective-permute-start(bf16[528,256]{1,0:T(8,128)(2,1)} %get-tuple-element.106), channel_id=1, source_target_pairs={{0,1},{1,2},{2,3},{3,0},{4,5},{5,6},{6,7},{7,4},{8,9},{9,10},{10,1... | collective-permute-start | bytes 811016 | tf_op jit(solution)/shard_map/ppermute | solution.py:409
  81.6 27.7 %collective-permute-start.13 = (bf16[528,256]{1,0:T(8,128)(2,1)}, bf16[528,256]{1,0:T(8,128)(2,1)S(1)}, u32[]{:S(2)}, u32[]{:S(2)}) collective-permute-start(bf16[528,256]{1,0:T(8,128)(2,1)} %get-tuple-element.110), channel_id=1, source_target_pairs={{0,3},{1,0},{2,1},{3,2},{4,7},{5,4},{6,5},{7,6},{8,11},{9,8},{10,9... | collective-permute-start | bytes 811016 | tf_op jit(solution)/shard_map/ppermute | solution.py:409
  84.9 3.1 %copy-start.13 = (bf16[528,256]{1,0:T(8,128)(2,1)}, bf16[528,256]{1,0:T(8,128)(2,1)S(1)}, u32[]{:S(2)}) copy-start(bf16[528,256]{1,0:T(8,128)(2,1)S(1)} %collective-permute-done.10.refs_9_) | copy-start | bytes 811012
  84.9 24.5 %collective-permute-start.8 = (bf16[528,256]{1,0:T(8,128)(2,1)}, bf16[528,256]{1,0:T(8,128)(2,1)S(1)}, u32[]{:S(2)}, u32[]{:S(2)}) collective-permute-start(bf16[528,256]{1,0:T(8,128)(2,1)} %get-tuple-element.104), channel_id=1, source_target_pairs={{0,1},{1,2},{2,3},{3,0},{4,5},{5,6},{6,7},{7,4},{8,9},{9,10},{10,1... | collective-permute-start | bytes 811016 | tf_op jit(solution)/shard_map/ppermute | solution.py:409
  84.9 24.5 %collective-permute-start.12 = (bf16[528,256]{1,0:T(8,128)(2,1)}, bf16[528,256]{1,0:T(8,128)(2,1)S(1)}, u32[]{:S(2)}, u32[]{:S(2)}) collective-permute-start(bf16[528,256]{1,0:T(8,128)(2,1)} %get-tuple-element.109), channel_id=1, source_target_pairs={{0,2},{1,3},{2,0},{3,1},{4,6},{5,7},{6,4},{7,5},{8,10},{9,11},{10,... | collective-permute-start | bytes 811016 | tf_op jit(solution)/shard_map/ppermute | solution.py:409
  106.4 27.9 %collective-permute-start.14 = (bf16[3,2,1024,128]{3,2,1,0:T(8,128)(2,1)}, bf16[3,2,1024,128]{3,2,1,0:T(8,128)(2,1)S(1)}, u32[]{:S(2)}, u32[]{:S(2)}) collective-permute-start(bf16[3,2,1024,128]{3,2,1,0:T(8,128)(2,1)} %get-tuple-element.131), channel_id=1, source_target_pairs={{4,0},{8,4},{12,8},{16,12},{20,16},{24,20},{28,24},{5,1},{9,5},{13... | collective-permute-start | bytes 4718600 | tf_op jit(solution)/shard_map/ppermute | solution.py:27
  120.8 13.5 %collective-permute-start.15 = (bf16[1,2,1024,128]{3,2,1,0:T(8,128)(2,1)}, bf16[1,2,1024,128]{3,2,1,0:T(8,128)(2,1)S(1)}, u32[]{:S(2)}, u32[]{:S(2)}) collective-permute-start(bf16[1,2,1024,128]{3,2,1,0:T(8,128)(2,1)} %get-tuple-element.132), channel_id=1, source_target_pairs={{4,0},{8,4},{12,8},{16,12},{20,16},{24,20},{28,24},{5,1},{9,5},{13... | collective-permute-start | bytes 1572872 | tf_op jit(solution)/shard_map/ppermute | solution.py:27
  (10 other events, 13.5 us)
where the time goes:
time: 141 us; the launch traced here: 140 us
  Pallas kernels  92.5 us (66%)
  starting transfers between devices  38.2 us (27%)
  local copies, waits for them, and re-layouts  5.01 us (4%)
  waiting for transfers between devices  2.96 us (2%)
    pallas_call x5, Pallas kernels, head_call(): pl.pallas_call(functools.partial(head_kernel, head, window, tok_rows, blo...  73.3 us
    ppermute x12, starting transfers between devices, sent(): return lax.ppermute(block, 'head', route)  26.1 us
    pallas_call x4, Pallas kernels, pack_call(): pl.pallas_call(functools.partial(pack_kernel, pieces, len(ends)), grid_sp...  12.6 us
    ppermute x4, starting transfers between devices, from_behind(): return lax.ppermute(block, axis, route)  12.1 us
    unnamed x36, local copies, waits for them, and re-layouts  5.01 us
    pallas_call x1, Pallas kernels, join_call(): pl.pallas_call(functools.partial(join_kernel, joint), grid=(kv_heads,), i...  4.45 us
  transfers between devices with their start and end apart: 16, of which 2 were waited for; matrix products, arithmetic and copies ran while one was open for 0% of the time, Pallas kernels for 60%

commit v1 on v0

--- a/solution.py
+++ b/solution.py
@@ -13,7 +13,7 @@
 BLOCK = 128
 SUB = 32
 UNROLL = 4
-VMEM_LIMIT = 60 * 1024 * 1024
+VMEM_LIMIT = 64 * 1024 * 1024 - 131072
 LOG2E = math.log2(math.e)
 F32 = jnp.float32
 BF16 = jnp.bfloat16

time: 141 us -> 139 us (0.986)
  local copies, waits for them, and re-layouts: 5.01 us -> 0.01 us
  starting transfers between devices: 38.2 us -> 40.6 us
    unnamed x36 -> x2, local copies, waits for them, and re-layouts: 5.01 us -> 0.01 us
    ppermute x12, starting transfers between devices: 26.1 us -> 27.6 us  [sent(): return lax.ppermute(block, 'head', route)]
    ppermute x12, waiting for transfers between devices: 2.05 us -> 3.53 us  [sent(): return lax.ppermute(block, 'head', route)]
  transfers between devices with their start and end apart: 16 -> 16, of which waited for: 2 -> 3; matrix products, arithmetic and copies ran while one was open for 0% -> 0% of each run, Pallas kernels for 60% -> 61%
where the time goes in v1:
time: 139 us
  Pallas kernels  92.4 us (66%)
  starting transfers between devices  40.6 us (29%)
  waiting for transfers between devices  4.29 us (3%)
    pallas_call x5, Pallas kernels, head_call(): pl.pallas_call(functools.partial(head_kernel, head, window, tok_rows, blo...  73.2 us
    ppermute x12, starting transfers between devices, sent(): return lax.ppermute(block, 'head', route)  27.6 us
    ppermute x4, starting transfers between devices, from_behind(): return lax.ppermute(block, axis, route)  13 us
    pallas_call x4, Pallas kernels, pack_call(): pl.pallas_call(functools.partial(pack_kernel, pieces, len(ends)), grid_sp...  12.6 us
    pallas_call x1, Pallas kernels, join_call(): pl.pallas_call(functools.partial(join_kernel, joint), grid=(kv_heads,), i...  4.46 us
    ppermute x12, waiting for transfers between devices, sent(): return lax.ppermute(block, 'head', route)  3.53 us
  transfers between devices with their start and end apart: 16, of which 3 were waited for; matrix products, arithmetic and copies ran while one was open for 0% of the time, Pallas kernels for 61%

profile of v1, /device:TPU:1, one launch (start us, length us, event | category | flops | bytes accessed | tf_op | source)
XLA Modules:
  0.0 138.6 jit_solution(13633278902519829431)
XLA Ops:
  0.6 3.7 %pack_cotangent.4 = (bf16[528,256]{1,0:T(8,128)(2,1)}, bf16[528,256]{1,0:T(8,128)(2,1)}, bf16[528,256]{1,0:T(8,128)(2,1)}, bf16[528,256]{1,0:T(8,128)(2,1)}, bf16[2,2,1024,128]{3,2,1,0:T(8,128)(2,1)}) custom-call(s32[1]{0:T(128)} %bitcast.me_ref, bf16[512,4096]{1,0:T(8,128)(2,1)} %refs_3_.7, bf16[512,4096]{1,0:T(8,128)(2,1)} %refs_3_.7, ...), custom_call_target="tpu_custom_call" | custom-call | flops 2097152 | bytes 3145728 | tf_op jit(solution)/shard_map/pack_cotangent/pallas_call | solution.py:84
  4.3 4.5 %collective-permute-start.1 = (bf16[2,2,1024,128]{3,2,1,0:T(8,128)(2,1)}, bf16[2,2,1024,128]{3,2,1,0:T(8,128)(2,1)}, u32[]{:S(2)}, u32[]{:S(2)}) collective-permute-start(bf16[2,2,1024,128]{3,2,1,0:T(8,128)(2,1)} %get-tuple-element.74), channel_id=1, source_target_pairs={{0,4},{4,8},{8,12},{12,16},{16,20},{20,24},{24,28},{1,5},{5,9},{9,... | collective-permute-start | bytes 3145736 | tf_op jit(solution)/shard_map/ppermute | solution.py:27
  8.8 1.3 collective-permute-start.2
  10.2 2.3 %collective-permute-start.3 = (bf16[528,256]{1,0:T(8,128)(2,1)}, bf16[528,256]{1,0:T(8,128)(2,1)}, u32[]{:S(2)}, u32[]{:S(2)}) collective-permute-start(bf16[528,256]{1,0:T(8,128)(2,1)} %get-tuple-element.79), channel_id=1, source_target_pairs={{0,2},{1,3},{2,0},{3,1},{4,6},{5,7},{6,4},{7,5},{8,10},{9,11},{10,... | collective-permute-start | bytes 811016 | tf_op jit(solution)/shard_map/ppermute | solution.py:409
  13.6 3.0 %pack_cotangent.5 = (bf16[528,256]{1,0:T(8,128)(2,1)}, bf16[528,256]{1,0:T(8,128)(2,1)}, bf16[528,256]{1,0:T(8,128)(2,1)}, bf16[528,256]{1,0:T(8,128)(2,1)}) custom-call(s32[1]{0:T(128)} %bitcast.me_ref, bf16[512,4096]{1,0:T(8,128)(2,1)} %refs_3_.7, bf16[512,4096]{1,0:T(8,128)(2,1)} %refs_3_.7, bf16[512,4096]{1,0:T(8,128)(2,1)} %refs_3_.7, ...), custom_call_target="tpu_custom_call" | custom-call | flops 2097152 | bytes 3145728 | tf_op jit(solution)/shard_map/pack_cotangent/pallas_call | solution.py:84
  16.5 3.0 %pack_cotangent.6 = (bf16[528,256]{1,0:T(8,128)(2,1)}, bf16[528,256]{1,0:T(8,128)(2,1)}, bf16[528,256]{1,0:T(8,128)(2,1)}, bf16[528,256]{1,0:T(8,128)(2,1)}) custom-call(s32[1]{0:T(128)} %bitcast.me_ref, bf16[512,4096]{1,0:T(8,128)(2,1)} %refs_3_.7, bf16[512,4096]{1,0:T(8,128)(2,1)} %refs_3_.7, bf16[512,4096]{1,0:T(8,128)(2,1)} %refs_3_.7, ...), custom_call_target="tpu_custom_call" | custom-call | flops 2097152 | bytes 3145728 | tf_op jit(solution)/shard_map/pack_cotangent/pallas_call | solution.py:84
  19.5 3.0 %pack_cotangent.7 = (bf16[528,256]{1,0:T(8,128)(2,1)}, bf16[528,256]{1,0:T(8,128)(2,1)}, bf16[528,256]{1,0:T(8,128)(2,1)}, bf16[528,256]{1,0:T(8,128)(2,1)}) custom-call(s32[1]{0:T(128)} %bitcast.me_ref, bf16[512,4096]{1,0:T(8,128)(2,1)} %refs_3_.7, bf16[512,4096]{1,0:T(8,128)(2,1)} %refs_3_.7, bf16[512,4096]{1,0:T(8,128)(2,1)} %refs_3_.7, ...), custom_call_target="tpu_custom_call" | custom-call | flops 2097152 | bytes 3145728 | tf_op jit(solution)/shard_map/pack_cotangent/pallas_call | solution.py:84
  22.5 2.1 %rims.1 = bf16[2,2,1024,128]{3,2,1,0:T(8,128)(2,1)} custom-call(bf16[4,2048,128]{2,1,0:T(8,128)(2,1)} %refs_2_.17, bf16[4,2048,128]{2,1,0:T(8,128)(2,1)} %refs_4_.17, bf16[528,256]{1,0:T(8,128)(2,1)} %get-tuple-element.81.after_ref.refs_7_), custom_call_target="tpu_custom_call" | custom-call | tf_op jit(solution)/shard_map/rims/pallas_call | solution.py:110
  24.6 2.7 %collective-permute-start = (bf16[2,2,1024,128]{3,2,1,0:T(8,128)(2,1)}, bf16[2,2,1024,128]{3,2,1,0:T(8,128)(2,1)}, u32[]{:S(2)}, u32[]{:S(2)}) collective-permute-start(bf16[2,2,1024,128]{3,2,1,0:T(8,128)(2,1)} %rims.1), channel_id=1, source_target_pairs={{0,4},{4,8},{8,12},{12,16},{16,20},{20,24},{24,28},{1,5},{5,9},{9,... | collective-permute-start | bytes 3145736 | tf_op jit(solution)/shard_map/ppermute | solution.py:27
  27.9 3.1 %collective-permute-done.3.refs_9_ = bf16[528,256]{1,0:T(8,128)(2,1)} collective-permute-done((bf16[528,256]{1,0:T(8,128)(2,1)}, bf16[528,256]{1,0:T(8,128)(2,1)}, u32[]{:S(2)}, u32[]{:S(2)}) %collective-permute-start.3) | collective-permute-done | bytes 270368 | tf_op jit(solution)/shard_map/ppermute | solution.py:409
  31.0 6.1 %collective-permute-start.5 = (bf16[528,256]{1,0:T(8,128)(2,1)}, bf16[528,256]{1,0:T(8,128)(2,1)}, u32[]{:S(2)}, u32[]{:S(2)}) collective-permute-start(bf16[528,256]{1,0:T(8,128)(2,1)} %get-tuple-element.89), channel_id=1, source_target_pairs={{0,1},{1,2},{2,3},{3,0},{4,5},{5,6},{6,7},{7,4},{8,9},{9,10},{10,1... | collective-permute-start | bytes 811016 | tf_op jit(solution)/shard_map/ppermute | solution.py:409
  37.1 1.3 collective-permute-start.6
  39.2 17.4 %head_backward.5 = (bf16[8,2048,128]{2,1,0:T(8,128)(2,1)}, bf16[4,2048,128]{2,1,0:T(8,128)(2,1)}, bf16[4,2048,128]{2,1,0:T(8,128)(2,1)}, bf16[4,1024,128]{2,1,0:...) custom-call(s32[1]{0:T(128)} %bitcast.me_ref, ...), custom_call_target="tpu_custom_call", output_to_operand_aliasing={{6}: (12, {}), {7}: (13, {}), {8}: (14, {})} | custom-call | flops 24159191040 | bytes 16384 | tf_op jit(solution)/shard_map/head_backward/pallas_call | solution.py:341
  57.0 5.1 %collective-permute-start.10 = (bf16[528,256]{1,0:T(8,128)(2,1)}, bf16[528,256]{1,0:T(8,128)(2,1)}, u32[]{:S(2)}, u32[]{:S(2)}) collective-permute-start(bf16[528,256]{1,0:T(8,128)(2,1)} %get-tuple-element.107), channel_id=1, source_target_pairs={{0,2},{1,3},{2,0},{3,1},{4,6},{5,7},{6,4},{7,5},{8,10},{9,11},{10,... | collective-permute-start | bytes 811016 | tf_op jit(solution)/shard_map/ppermute | solution.py:409
  62.0 3.1 %collective-permute-start.11 = (bf16[528,256]{1,0:T(8,128)(2,1)}, bf16[528,256]{1,0:T(8,128)(2,1)}, u32[]{:S(2)}, u32[]{:S(2)}) collective-permute-start(bf16[528,256]{1,0:T(8,128)(2,1)} %get-tuple-element.108), channel_id=1, source_target_pairs={{0,3},{1,0},{2,1},{3,2},{4,7},{5,4},{6,5},{7,6},{8,11},{9,8},{10,9... | collective-permute-start | bytes 811016 | tf_op jit(solution)/shard_map/ppermute | solution.py:409
  65.1 17.4 %head_backward.6 = (bf16[8,2048,128]{2,1,0:T(8,128)(2,1)}, bf16[4,2048,128]{2,1,0:T(8,128)(2,1)}, bf16[4,2048,128]{2,1,0:T(8,128)(2,1)}, bf16[4,1024,128]{2,1,0:...) custom-call(s32[1]{0:T(128)} %bitcast.me_ref, ...), custom_call_target="tpu_custom_call", output_to_operand_aliasing={{0}: (12, {}), {1}: (13, {}), {2}: (14, {}), {3}: (15, {}),... | custom-call | flops 24159191040 | bytes 16384 | tf_op jit(solution)/shard_map/head_backward/pallas_call | solution.py:341
  82.5 3.3 %collective-permute-start.13 = (bf16[528,256]{1,0:T(8,128)(2,1)}, bf16[528,256]{1,0:T(8,128)(2,1)}, u32[]{:S(2)}, u32[]{:S(2)}) collective-permute-start(bf16[528,256]{1,0:T(8,128)(2,1)} %get-tuple-element.110), channel_id=1, source_target_pairs={{0,3},{1,0},{2,1},{3,2},{4,7},{5,4},{6,5},{7,6},{8,11},{9,8},{10,9... | collective-permute-start | bytes 811016 | tf_op jit(solution)/shard_map/ppermute | solution.py:409
  85.8 3.3 %collective-permute-start.12 = (bf16[528,256]{1,0:T(8,128)(2,1)}, bf16[528,256]{1,0:T(8,128)(2,1)}, u32[]{:S(2)}, u32[]{:S(2)}) collective-permute-start(bf16[528,256]{1,0:T(8,128)(2,1)} %get-tuple-element.109), channel_id=1, source_target_pairs={{0,2},{1,3},{2,0},{3,1},{4,6},{5,7},{6,4},{7,5},{8,10},{9,11},{10,... | collective-permute-start | bytes 811016 | tf_op jit(solution)/shard_map/ppermute | solution.py:409
  89.1 17.4 %head_backward.7 = (bf16[8,2048,128]{2,1,0:T(8,128)(2,1)}, bf16[4,2048,128]{2,1,0:T(8,128)(2,1)}, bf16[4,2048,128]{2,1,0:T(8,128)(2,1)}, bf16[4,1024,128]{2,1,0:...) custom-call(s32[1]{0:T(128)} %bitcast.me_ref, ...), custom_call_target="tpu_custom_call", output_to_operand_aliasing={{0}: (12, {}), {1}: (13, {}), {2}: (14, {}), {3}: (15, {}),... | custom-call | flops 24159191040 | bytes 16384 | tf_op jit(solution)/shard_map/head_backward/pallas_call | solution.py:341
  106.5 3.0 %collective-permute-start.14 = (bf16[3,2,1024,128]{3,2,1,0:T(8,128)(2,1)}, bf16[3,2,1024,128]{3,2,1,0:T(8,128)(2,1)}, u32[]{:S(2)}, u32[]{:S(2)}) collective-permute-start(bf16[3,2,1024,128]{3,2,1,0:T(8,128)(2,1)} %get-tuple-element.131), channel_id=1, source_target_pairs={{4,0},{8,4},{12,8},{16,12},{20,16},{24,20},{28,24},{5,1},{9,5},{13... | collective-permute-start | bytes 4718600 | tf_op jit(solution)/shard_map/ppermute | solution.py:27
  109.5 10.5 %head_backward.8 = (bf16[8,2048,128]{2,1,0:T(8,128)(2,1)}, f32[1024,128]{1,0:T(8,128)}, f32[1024,128]{1,0:T(8,128)}, bf16[1,2,1024,128]{3,2,1,0:T(8,128)(2,1)}) custom-call(s32[1]{0:T(128)} %bitcast.me_ref, bf16[8,2048,128]{2,1,0:T(8,128)(2,1)} %refs_0_.17, ...), custom_call_target="tpu_custom_call", output_to_operand_aliasing={{0}: (12, {})} | custom-call | flops 12079595520 | bytes 16384 | tf_op jit(solution)/shard_map/head_backward/pallas_call | solution.py:341
  120.0 2.7 %collective-permute-start.15 = (bf16[1,2,1024,128]{3,2,1,0:T(8,128)(2,1)}, bf16[1,2,1024,128]{3,2,1,0:T(8,128)(2,1)}, u32[]{:S(2)}, u32[]{:S(2)}) collective-permute-start(bf16[1,2,1024,128]{3,2,1,0:T(8,128)(2,1)} %get-tuple-element.132), channel_id=1, source_target_pairs={{4,0},{8,4},{12,8},{16,12},{20,16},{24,20},{28,24},{5,1},{9,5},{13... | collective-permute-start | bytes 1572872 | tf_op jit(solution)/shard_map/ppermute | solution.py:27
  122.7 10.7 %head_backward.9 = (bf16[8,2048,128]{2,1,0:T(8,128)(2,1)}, bf16[4,2048,128]{2,1,0:T(8,128)(2,1)}, bf16[4,2048,128]{2,1,0:T(8,128)(2,1)}, bf16[4,1024,128]{2,1,0:T(8,128)(2,1)}, bf16[4,1024,128]{2,1,0:T(8,128)(2,1)}) custom-call(s32[1]{0:T(128)} %bitcast.me_ref, ...), custom_call_target="tpu_custom_call", output_to_operand_aliasing={{0}: (14, {}), {1}: (15, {}), {2}: (16, {}), {3}: (17, {}),... | custom-call | flops 12079595520 | bytes 16384 | tf_op jit(solution)/shard_map/head_backward/pallas_call | solution.py:341
  134.1 4.5 %join_tails.1 = (bf16[4,2048,128]{2,1,0:T(8,128)(2,1)}, bf16[4,2048,128]{2,1,0:T(8,128)(2,1)}) custom-call(bf16[4,1024,128]{2,1,0:T(8,128)(2,1)} %get-tuple-element.129.dk_tail_ref, bf16[4,1024,128]{2,1,0:T(8,128)(2,1)} %get-tuple-element.130.dv_tail_ref, ...), custom_call_target="tpu_custom_call", output_to_operand_aliasing={{0}: (4, {}), {1}: (5, {})} | custom-call | tf_op jit(solution)/shard_map/join_tails/pallas_call | solution.py:387
  (22 shorter events, 3.7 us)
Async XLA Ops:
  4.3 34.9 %collective-permute-start.1 = (bf16[2,2,1024,128]{3,2,1,0:T(8,128)(2,1)}, bf16[2,2,1024,128]{3,2,1,0:T(8,128)(2,1)}, u32[]{:S(2)}, u32[]{:S(2)}) collective-permute-start(bf16[2,2,1024,128]{3,2,1,0:T(8,128)(2,1)} %get-tuple-element.74), channel_id=1, source_target_pairs={{0,4},{4,8},{8,12},{12,16},{16,20},{20,24},{24,28},{1,5},{5,9},{9,... | collective-permute-start | bytes 3145736 | tf_op jit(solution)/shard_map/ppermute | solution.py:27
  8.8 19.1 %collective-permute-start.2 = (bf16[528,256]{1,0:T(8,128)(2,1)}, bf16[528,256]{1,0:T(8,128)(2,1)}, u32[]{:S(2)}, u32[]{:S(2)}) collective-permute-start(bf16[528,256]{1,0:T(8,128)(2,1)} %get-tuple-element.78), channel_id=1, source_target_pairs={{0,1},{1,2},{2,3},{3,0},{4,5},{5,6},{6,7},{7,4},{8,9},{9,10},{10,1... | collective-permute-start | bytes 811016 | tf_op jit(solution)/shard_map/ppermute | solution.py:409
  10.2 20.9 %collective-permute-start.3 = (bf16[528,256]{1,0:T(8,128)(2,1)}, bf16[528,256]{1,0:T(8,128)(2,1)}, u32[]{:S(2)}, u32[]{:S(2)}) collective-permute-start(bf16[528,256]{1,0:T(8,128)(2,1)} %get-tuple-element.79), channel_id=1, source_target_pairs={{0,2},{1,3},{2,0},{3,1},{4,6},{5,7},{6,4},{7,5},{8,10},{9,11},{10,... | collective-permute-start | bytes 811016 | tf_op jit(solution)/shard_map/ppermute | solution.py:409
  12.5 18.6 %collective-permute-start.4 = (bf16[528,256]{1,0:T(8,128)(2,1)}, bf16[528,256]{1,0:T(8,128)(2,1)}, u32[]{:S(2)}, u32[]{:S(2)}) collective-permute-start(bf16[528,256]{1,0:T(8,128)(2,1)} %get-tuple-element.80), channel_id=1, source_target_pairs={{0,3},{1,0},{2,1},{3,2},{4,7},{5,4},{6,5},{7,6},{8,11},{9,8},{10,9... | collective-permute-start | bytes 811016 | tf_op jit(solution)/shard_map/ppermute | solution.py:409
  22.5 4.8 %copy-start = (s32[2048]{0:T(1024)S(1)}, s32[2048]{0:T(1024)}, u32[]{:S(2)}) copy-start(s32[2048]{0:T(1024)} %param.13) | copy-start | bytes 24580
  24.6 64.5 %collective-permute-start = (bf16[2,2,1024,128]{3,2,1,0:T(8,128)(2,1)}, bf16[2,2,1024,128]{3,2,1,0:T(8,128)(2,1)}, u32[]{:S(2)}, u32[]{:S(2)}) collective-permute-start(bf16[2,2,1024,128]{3,2,1,0:T(8,128)(2,1)} %rims.1), channel_id=1, source_target_pairs={{0,4},{4,8},{8,12},{12,16},{16,20},{20,24},{24,28},{1,5},{5,9},{9,... | collective-permute-start | bytes 3145736 | tf_op jit(solution)/shard_map/ppermute | solution.py:27
  31.0 25.5 %collective-permute-start.5 = (bf16[528,256]{1,0:T(8,128)(2,1)}, bf16[528,256]{1,0:T(8,128)(2,1)}, u32[]{:S(2)}, u32[]{:S(2)}) collective-permute-start(bf16[528,256]{1,0:T(8,128)(2,1)} %get-tuple-element.89), channel_id=1, source_target_pairs={{0,1},{1,2},{2,3},{3,0},{4,5},{5,6},{6,7},{7,4},{8,9},{9,10},{10,1... | collective-permute-start | bytes 811016 | tf_op jit(solution)/shard_map/ppermute | solution.py:409
  37.1 19.9 %collective-permute-start.6 = (bf16[528,256]{1,0:T(8,128)(2,1)}, bf16[528,256]{1,0:T(8,128)(2,1)}, u32[]{:S(2)}, u32[]{:S(2)}) collective-permute-start(bf16[528,256]{1,0:T(8,128)(2,1)} %get-tuple-element.90), channel_id=1, source_target_pairs={{0,2},{1,3},{2,0},{3,1},{4,6},{5,7},{6,4},{7,5},{8,10},{9,11},{10,... | collective-permute-start | bytes 811016 | tf_op jit(solution)/shard_map/ppermute | solution.py:409
  38.4 18.6 %collective-permute-start.7 = (bf16[528,256]{1,0:T(8,128)(2,1)}, bf16[528,256]{1,0:T(8,128)(2,1)}, u32[]{:S(2)}, u32[]{:S(2)}) collective-permute-start(bf16[528,256]{1,0:T(8,128)(2,1)} %get-tuple-element.91), channel_id=1, source_target_pairs={{0,3},{1,0},{2,1},{3,2},{4,7},{5,4},{6,5},{7,6},{8,11},{9,8},{10,9... | collective-permute-start | bytes 811016 | tf_op jit(solution)/shard_map/ppermute | solution.py:409
  57.0 28.8 %collective-permute-start.10 = (bf16[528,256]{1,0:T(8,128)(2,1)}, bf16[528,256]{1,0:T(8,128)(2,1)}, u32[]{:S(2)}, u32[]{:S(2)}) collective-permute-start(bf16[528,256]{1,0:T(8,128)(2,1)} %get-tuple-element.107), channel_id=1, source_target_pairs={{0,2},{1,3},{2,0},{3,1},{4,6},{5,7},{6,4},{7,5},{8,10},{9,11},{10,... | collective-permute-start | bytes 811016 | tf_op jit(solution)/shard_map/ppermute | solution.py:409
  62.0 23.7 %collective-permute-start.11 = (bf16[528,256]{1,0:T(8,128)(2,1)}, bf16[528,256]{1,0:T(8,128)(2,1)}, u32[]{:S(2)}, u32[]{:S(2)}) collective-permute-start(bf16[528,256]{1,0:T(8,128)(2,1)} %get-tuple-element.108), channel_id=1, source_target_pairs={{0,3},{1,0},{2,1},{3,2},{4,7},{5,4},{6,5},{7,6},{8,11},{9,8},{10,9... | collective-permute-start | bytes 811016 | tf_op jit(solution)/shard_map/ppermute | solution.py:409
  65.1 20.6 %collective-permute-start.9 = (bf16[528,256]{1,0:T(8,128)(2,1)}, bf16[528,256]{1,0:T(8,128)(2,1)}, u32[]{:S(2)}, u32[]{:S(2)}) collective-permute-start(bf16[528,256]{1,0:T(8,128)(2,1)} %get-tuple-element.106), channel_id=1, source_target_pairs={{0,1},{1,2},{2,3},{3,0},{4,5},{5,6},{6,7},{7,4},{8,9},{9,10},{10,1... | collective-permute-start | bytes 811016 | tf_op jit(solution)/shard_map/ppermute | solution.py:409
  82.5 27.0 %collective-permute-start.13 = (bf16[528,256]{1,0:T(8,128)(2,1)}, bf16[528,256]{1,0:T(8,128)(2,1)}, u32[]{:S(2)}, u32[]{:S(2)}) collective-permute-start(bf16[528,256]{1,0:T(8,128)(2,1)} %get-tuple-element.110), channel_id=1, source_target_pairs={{0,3},{1,0},{2,1},{3,2},{4,7},{5,4},{6,5},{7,6},{8,11},{9,8},{10,9... | collective-permute-start | bytes 811016 | tf_op jit(solution)/shard_map/ppermute | solution.py:409
  85.8 23.7 %collective-permute-start.8 = (bf16[528,256]{1,0:T(8,128)(2,1)}, bf16[528,256]{1,0:T(8,128)(2,1)}, u32[]{:S(2)}, u32[]{:S(2)}) collective-permute-start(bf16[528,256]{1,0:T(8,128)(2,1)} %get-tuple-element.104), channel_id=1, source_target_pairs={{0,1},{1,2},{2,3},{3,0},{4,5},{5,6},{6,7},{7,4},{8,9},{9,10},{10,1... | collective-permute-start | bytes 811016 | tf_op jit(solution)/shard_map/ppermute | solution.py:409
  85.8 23.7 %collective-permute-start.12 = (bf16[528,256]{1,0:T(8,128)(2,1)}, bf16[528,256]{1,0:T(8,128)(2,1)}, u32[]{:S(2)}, u32[]{:S(2)}) collective-permute-start(bf16[528,256]{1,0:T(8,128)(2,1)} %get-tuple-element.109), channel_id=1, source_target_pairs={{0,2},{1,3},{2,0},{3,1},{4,6},{5,7},{6,4},{7,5},{8,10},{9,11},{10,... | collective-permute-start | bytes 811016 | tf_op jit(solution)/shard_map/ppermute | solution.py:409
  106.5 27.7 %collective-permute-start.14 = (bf16[3,2,1024,128]{3,2,1,0:T(8,128)(2,1)}, bf16[3,2,1024,128]{3,2,1,0:T(8,128)(2,1)}, u32[]{:S(2)}, u32[]{:S(2)}) collective-permute-start(bf16[3,2,1024,128]{3,2,1,0:T(8,128)(2,1)} %get-tuple-element.131), channel_id=1, source_target_pairs={{4,0},{8,4},{12,8},{16,12},{20,16},{24,20},{28,24},{5,1},{9,5},{13... | collective-permute-start | bytes 4718600 | tf_op jit(solution)/shard_map/ppermute | solution.py:27
  120.0 14.2 %collective-permute-start.15 = (bf16[1,2,1024,128]{3,2,1,0:T(8,128)(2,1)}, bf16[1,2,1024,128]{3,2,1,0:T(8,128)(2,1)}, u32[]{:S(2)}, u32[]{:S(2)}) collective-permute-start(bf16[1,2,1024,128]{3,2,1,0:T(8,128)(2,1)} %get-tuple-element.132), channel_id=1, source_target_pairs={{4,0},{8,4},{12,8},{16,12},{20,16},{24,20},{28,24},{5,1},{9,5},{13... | collective-permute-start | bytes 1572872 | tf_op jit(solution)/shard_map/ppermute | solution.py:27

commit v2 on v1

--- a/solution.py
+++ b/solution.py
@@ -305,7 +305,7 @@
     in_specs += [full(*array.shape) for array in carry]
     n_in = 1 + 7 + pieces + len(carry)
     aliases = {n_in + i: i for i in range(len(before))}
-    unroll = math.gcd(UNROLL, count)
+    unroll = count if count <= 2 * UNROLL else math.gcd(UNROLL, count)
     out_specs = [q_spec]
     out_shape = [jax.ShapeDtypeStruct(queries.shape, BF16)]
     if first_block + count == tok_rows // BLOCK:

time: 139 us -> 139 us (level)
  transfers between devices with their start and end apart: 16 -> 16, of which waited for: 3 -> 3; matrix products, arithmetic and copies ran while one was open for 0% -> 0% of each run, Pallas kernels for 61% -> 60%
where the time goes in v2:
time: 139 us
  Pallas kernels  91.1 us (66%)
  starting transfers between devices  40.8 us (29%)
  waiting for transfers between devices  5.32 us (4%)
    pallas_call x5, Pallas kernels, head_call(): pl.pallas_call(functools.partial(head_kernel, head, window, tok_rows, blo...  71.9 us
    ppermute x12, starting transfers between devices, sent(): return lax.ppermute(block, 'head', route)  27.6 us
    ppermute x4, starting transfers between devices, from_behind(): return lax.ppermute(block, axis, route)  13.2 us
    pallas_call x4, Pallas kernels, pack_call(): pl.pallas_call(functools.partial(pack_kernel, pieces, len(ends)), grid_sp...  12.6 us
    pallas_call x1, Pallas kernels, join_call(): pl.pallas_call(functools.partial(join_kernel, joint), grid=(kv_heads,), i...  4.46 us
    ppermute x12, waiting for transfers between devices, sent(): return lax.ppermute(block, 'head', route)  3.53 us
  transfers between devices with their start and end apart: 16, of which 3 were waited for; matrix products, arithmetic and copies ran while one was open for 0% of the time, Pallas kernels for 60%

profile of v2, /device:TPU:1, one launch (start us, length us, event | category | flops | bytes accessed | tf_op | source)
XLA Modules:
  0.0 138.6 jit_solution(8301534431330508388)
XLA Ops:
  0.6 3.7 %pack_cotangent.4 = (bf16[528,256]{1,0:T(8,128)(2,1)}, bf16[528,256]{1,0:T(8,128)(2,1)}, bf16[528,256]{1,0:T(8,128)(2,1)}, bf16[528,256]{1,0:T(8,128)(2,1)}, bf16[2,2,1024,128]{3,2,1,0:T(8,128)(2,1)}) custom-call(s32[1]{0:T(128)} %bitcast.me_ref, bf16[512,4096]{1,0:T(8,128)(2,1)} %refs_3_.7, bf16[512,4096]{1,0:T(8,128)(2,1)} %refs_3_.7, ...), custom_call_target="tpu_custom_call" | custom-call | flops 2097152 | bytes 3145728 | tf_op jit(solution)/shard_map/pack_cotangent/pallas_call | solution.py:84
  4.3 4.5 %collective-permute-start.1 = (bf16[2,2,1024,128]{3,2,1,0:T(8,128)(2,1)}, bf16[2,2,1024,128]{3,2,1,0:T(8,128)(2,1)}, u32[]{:S(2)}, u32[]{:S(2)}) collective-permute-start(bf16[2,2,1024,128]{3,2,1,0:T(8,128)(2,1)} %get-tuple-element.74), channel_id=1, source_target_pairs={{0,4},{4,8},{8,12},{12,16},{16,20},{20,24},{24,28},{1,5},{5,9},{9,... | collective-permute-start | bytes 3145736 | tf_op jit(solution)/shard_map/ppermute | solution.py:27
  8.8 1.3 collective-permute-start.2
  10.2 2.3 %collective-permute-start.3 = (bf16[528,256]{1,0:T(8,128)(2,1)}, bf16[528,256]{1,0:T(8,128)(2,1)}, u32[]{:S(2)}, u32[]{:S(2)}) collective-permute-start(bf16[528,256]{1,0:T(8,128)(2,1)} %get-tuple-element.79), channel_id=1, source_target_pairs={{0,2},{1,3},{2,0},{3,1},{4,6},{5,7},{6,4},{7,5},{8,10},{9,11},{10,... | collective-permute-start | bytes 811016 | tf_op jit(solution)/shard_map/ppermute | solution.py:409
  13.6 3.0 %pack_cotangent.5 = (bf16[528,256]{1,0:T(8,128)(2,1)}, bf16[528,256]{1,0:T(8,128)(2,1)}, bf16[528,256]{1,0:T(8,128)(2,1)}, bf16[528,256]{1,0:T(8,128)(2,1)}) custom-call(s32[1]{0:T(128)} %bitcast.me_ref, bf16[512,4096]{1,0:T(8,128)(2,1)} %refs_3_.7, bf16[512,4096]{1,0:T(8,128)(2,1)} %refs_3_.7, bf16[512,4096]{1,0:T(8,128)(2,1)} %refs_3_.7, ...), custom_call_target="tpu_custom_call" | custom-call | flops 2097152 | bytes 3145728 | tf_op jit(solution)/shard_map/pack_cotangent/pallas_call | solution.py:84
  16.5 3.0 %pack_cotangent.6 = (bf16[528,256]{1,0:T(8,128)(2,1)}, bf16[528,256]{1,0:T(8,128)(2,1)}, bf16[528,256]{1,0:T(8,128)(2,1)}, bf16[528,256]{1,0:T(8,128)(2,1)}) custom-call(s32[1]{0:T(128)} %bitcast.me_ref, bf16[512,4096]{1,0:T(8,128)(2,1)} %refs_3_.7, bf16[512,4096]{1,0:T(8,128)(2,1)} %refs_3_.7, bf16[512,4096]{1,0:T(8,128)(2,1)} %refs_3_.7, ...), custom_call_target="tpu_custom_call" | custom-call | flops 2097152 | bytes 3145728 | tf_op jit(solution)/shard_map/pack_cotangent/pallas_call | solution.py:84
  19.5 3.0 %pack_cotangent.7 = (bf16[528,256]{1,0:T(8,128)(2,1)}, bf16[528,256]{1,0:T(8,128)(2,1)}, bf16[528,256]{1,0:T(8,128)(2,1)}, bf16[528,256]{1,0:T(8,128)(2,1)}) custom-call(s32[1]{0:T(128)} %bitcast.me_ref, bf16[512,4096]{1,0:T(8,128)(2,1)} %refs_3_.7, bf16[512,4096]{1,0:T(8,128)(2,1)} %refs_3_.7, bf16[512,4096]{1,0:T(8,128)(2,1)} %refs_3_.7, ...), custom_call_target="tpu_custom_call" | custom-call | flops 2097152 | bytes 3145728 | tf_op jit(solution)/shard_map/pack_cotangent/pallas_call | solution.py:84
  22.5 2.1 %rims.1 = bf16[2,2,1024,128]{3,2,1,0:T(8,128)(2,1)} custom-call(bf16[4,2048,128]{2,1,0:T(8,128)(2,1)} %refs_2_.17, bf16[4,2048,128]{2,1,0:T(8,128)(2,1)} %refs_4_.17, bf16[528,256]{1,0:T(8,128)(2,1)} %get-tuple-element.81.after_ref.refs_7_), custom_call_target="tpu_custom_call" | custom-call | tf_op jit(solution)/shard_map/rims/pallas_call | solution.py:110
  24.6 2.7 %collective-permute-start = (bf16[2,2,1024,128]{3,2,1,0:T(8,128)(2,1)}, bf16[2,2,1024,128]{3,2,1,0:T(8,128)(2,1)}, u32[]{:S(2)}, u32[]{:S(2)}) collective-permute-start(bf16[2,2,1024,128]{3,2,1,0:T(8,128)(2,1)} %rims.1), channel_id=1, source_target_pairs={{0,4},{4,8},{8,12},{12,16},{16,20},{20,24},{24,28},{1,5},{5,9},{9,... | collective-permute-start | bytes 3145736 | tf_op jit(solution)/shard_map/ppermute | solution.py:27
  27.9 3.1 %collective-permute-done.3.refs_9_ = bf16[528,256]{1,0:T(8,128)(2,1)} collective-permute-done((bf16[528,256]{1,0:T(8,128)(2,1)}, bf16[528,256]{1,0:T(8,128)(2,1)}, u32[]{:S(2)}, u32[]{:S(2)}) %collective-permute-start.3) | collective-permute-done | bytes 270368 | tf_op jit(solution)/shard_map/ppermute | solution.py:409
  31.0 6.1 %collective-permute-start.5 = (bf16[528,256]{1,0:T(8,128)(2,1)}, bf16[528,256]{1,0:T(8,128)(2,1)}, u32[]{:S(2)}, u32[]{:S(2)}) collective-permute-start(bf16[528,256]{1,0:T(8,128)(2,1)} %get-tuple-element.89), channel_id=1, source_target_pairs={{0,1},{1,2},{2,3},{3,0},{4,5},{5,6},{6,7},{7,4},{8,9},{9,10},{10,1... | collective-permute-start | bytes 811016 | tf_op jit(solution)/shard_map/ppermute | solution.py:409
  39.2 17.4 %head_backward.5 = (bf16[8,2048,128]{2,1,0:T(8,128)(2,1)}, bf16[4,2048,128]{2,1,0:T(8,128)(2,1)}, bf16[4,2048,128]{2,1,0:T(8,128)(2,1)}, bf16[4,1024,128]{2,1,0:...) custom-call(s32[1]{0:T(128)} %bitcast.me_ref, ...), custom_call_target="tpu_custom_call", output_to_operand_aliasing={{6}: (12, {}), {7}: (13, {}), {8}: (14, {})} | custom-call | flops 24159191040 | bytes 16384 | tf_op jit(solution)/shard_map/head_backward/pallas_call | solution.py:341
  57.0 5.1 %collective-permute-start.10 = (bf16[528,256]{1,0:T(8,128)(2,1)}, bf16[528,256]{1,0:T(8,128)(2,1)}, u32[]{:S(2)}, u32[]{:S(2)}) collective-permute-start(bf16[528,256]{1,0:T(8,128)(2,1)} %get-tuple-element.107), channel_id=1, source_target_pairs={{0,2},{1,3},{2,0},{3,1},{4,6},{5,7},{6,4},{7,5},{8,10},{9,11},{10,... | collective-permute-start | bytes 811016 | tf_op jit(solution)/shard_map/ppermute | solution.py:409
  62.0 3.1 %collective-permute-start.11 = (bf16[528,256]{1,0:T(8,128)(2,1)}, bf16[528,256]{1,0:T(8,128)(2,1)}, u32[]{:S(2)}, u32[]{:S(2)}) collective-permute-start(bf16[528,256]{1,0:T(8,128)(2,1)} %get-tuple-element.108), channel_id=1, source_target_pairs={{0,3},{1,0},{2,1},{3,2},{4,7},{5,4},{6,5},{7,6},{8,11},{9,8},{10,9... | collective-permute-start | bytes 811016 | tf_op jit(solution)/shard_map/ppermute | solution.py:409
  65.1 17.4 %head_backward.6 = (bf16[8,2048,128]{2,1,0:T(8,128)(2,1)}, bf16[4,2048,128]{2,1,0:T(8,128)(2,1)}, bf16[4,2048,128]{2,1,0:T(8,128)(2,1)}, bf16[4,1024,128]{2,1,0:...) custom-call(s32[1]{0:T(128)} %bitcast.me_ref, ...), custom_call_target="tpu_custom_call", output_to_operand_aliasing={{0}: (12, {}), {1}: (13, {}), {2}: (14, {}), {3}: (15, {}),... | custom-call | flops 24159191040 | bytes 16384 | tf_op jit(solution)/shard_map/head_backward/pallas_call | solution.py:341
  82.5 3.3 %collective-permute-start.13 = (bf16[528,256]{1,0:T(8,128)(2,1)}, bf16[528,256]{1,0:T(8,128)(2,1)}, u32[]{:S(2)}, u32[]{:S(2)}) collective-permute-start(bf16[528,256]{1,0:T(8,128)(2,1)} %get-tuple-element.110), channel_id=1, source_target_pairs={{0,3},{1,0},{2,1},{3,2},{4,7},{5,4},{6,5},{7,6},{8,11},{9,8},{10,9... | collective-permute-start | bytes 811016 | tf_op jit(solution)/shard_map/ppermute | solution.py:409
  85.8 3.3 %collective-permute-start.12 = (bf16[528,256]{1,0:T(8,128)(2,1)}, bf16[528,256]{1,0:T(8,128)(2,1)}, u32[]{:S(2)}, u32[]{:S(2)}) collective-permute-start(bf16[528,256]{1,0:T(8,128)(2,1)} %get-tuple-element.109), channel_id=1, source_target_pairs={{0,2},{1,3},{2,0},{3,1},{4,6},{5,7},{6,4},{7,5},{8,10},{9,11},{10,... | collective-permute-start | bytes 811016 | tf_op jit(solution)/shard_map/ppermute | solution.py:409
  89.1 17.4 %head_backward.7 = (bf16[8,2048,128]{2,1,0:T(8,128)(2,1)}, bf16[4,2048,128]{2,1,0:T(8,128)(2,1)}, bf16[4,2048,128]{2,1,0:T(8,128)(2,1)}, bf16[4,1024,128]{2,1,0:...) custom-call(s32[1]{0:T(128)} %bitcast.me_ref, ...), custom_call_target="tpu_custom_call", output_to_operand_aliasing={{0}: (12, {}), {1}: (13, {}), {2}: (14, {}), {3}: (15, {}),... | custom-call | flops 24159191040 | bytes 16384 | tf_op jit(solution)/shard_map/head_backward/pallas_call | solution.py:341
  106.5 3.0 %collective-permute-start.14 = (bf16[3,2,1024,128]{3,2,1,0:T(8,128)(2,1)}, bf16[3,2,1024,128]{3,2,1,0:T(8,128)(2,1)}, u32[]{:S(2)}, u32[]{:S(2)}) collective-permute-start(bf16[3,2,1024,128]{3,2,1,0:T(8,128)(2,1)} %get-tuple-element.131), channel_id=1, source_target_pairs={{4,0},{8,4},{12,8},{16,12},{20,16},{24,20},{28,24},{5,1},{9,5},{13... | collective-permute-start | bytes 4718600 | tf_op jit(solution)/shard_map/ppermute | solution.py:27
  109.5 9.8 %head_backward.8 = (bf16[8,2048,128]{2,1,0:T(8,128)(2,1)}, f32[1024,128]{1,0:T(8,128)}, f32[1024,128]{1,0:T(8,128)}, bf16[1,2,1024,128]{3,2,1,0:T(8,128)(2,1)}) custom-call(s32[1]{0:T(128)} %bitcast.me_ref, bf16[8,2048,128]{2,1,0:T(8,128)(2,1)} %refs_0_.17, ...), custom_call_target="tpu_custom_call", output_to_operand_aliasing={{0}: (12, {})} | custom-call | flops 12079595520 | bytes 16384 | tf_op jit(solution)/shard_map/head_backward/pallas_call | solution.py:341
  119.3 3.0 %collective-permute-start.15 = (bf16[1,2,1024,128]{3,2,1,0:T(8,128)(2,1)}, bf16[1,2,1024,128]{3,2,1,0:T(8,128)(2,1)}, u32[]{:S(2)}, u32[]{:S(2)}) collective-permute-start(bf16[1,2,1024,128]{3,2,1,0:T(8,128)(2,1)} %get-tuple-element.132), channel_id=1, source_target_pairs={{4,0},{8,4},{12,8},{16,12},{20,16},{24,20},{28,24},{5,1},{9,5},{13... | collective-permute-start | bytes 1572872 | tf_op jit(solution)/shard_map/ppermute | solution.py:27
  122.3 10.0 %head_backward.9 = (bf16[8,2048,128]{2,1,0:T(8,128)(2,1)}, bf16[4,2048,128]{2,1,0:T(8,128)(2,1)}, bf16[4,2048,128]{2,1,0:T(8,128)(2,1)}, bf16[4,1024,128]{2,1,0:T(8,128)(2,1)}, bf16[4,1024,128]{2,1,0:T(8,128)(2,1)}) custom-call(s32[1]{0:T(128)} %bitcast.me_ref, ...), custom_call_target="tpu_custom_call", output_to_operand_aliasing={{0}: (14, {}), {1}: (15, {}), {2}: (16, {}), {3}: (17, {}),... | custom-call | flops 12079595520 | bytes 16384 | tf_op jit(solution)/shard_map/head_backward/pallas_call | solution.py:341
  132.3 1.8 %collective-permute-done.15.refs_1_ = bf16[1,2,1024,128]{3,2,1,0:T(8,128)(2,1)} collective-permute-done((bf16[1,2,1024,128]{3,2,1,0:T(8,128)(2,1)}, bf16[1,2,1024,128]{3,2,1,0:T(8,128)(2,1)}, u32[]{:S(2)}, u32[]{:S(2)}) %collective-permute-start.15) | collective-permute-done | bytes 524320 | tf_op jit(solution)/shard_map/ppermute | solution.py:27
  134.1 4.5 %join_tails.1 = (bf16[4,2048,128]{2,1,0:T(8,128)(2,1)}, bf16[4,2048,128]{2,1,0:T(8,128)(2,1)}) custom-call(bf16[4,1024,128]{2,1,0:T(8,128)(2,1)} %get-tuple-element.129.dk_tail_ref, bf16[4,1024,128]{2,1,0:T(8,128)(2,1)} %get-tuple-element.130.dv_tail_ref, ...), custom_call_target="tpu_custom_call", output_to_operand_aliasing={{0}: (4, {}), {1}: (5, {})} | custom-call | tf_op jit(solution)/shard_map/join_tails/pallas_call | solution.py:387
  (22 shorter events, 4.2 us)
Async XLA Ops:
  4.3 34.9 %collective-permute-start.1 = (bf16[2,2,1024,128]{3,2,1,0:T(8,128)(2,1)}, bf16[2,2,1024,128]{3,2,1,0:T(8,128)(2,1)}, u32[]{:S(2)}, u32[]{:S(2)}) collective-permute-start(bf16[2,2,1024,128]{3,2,1,0:T(8,128)(2,1)} %get-tuple-element.74), channel_id=1, source_target_pairs={{0,4},{4,8},{8,12},{12,16},{16,20},{20,24},{24,28},{1,5},{5,9},{9,... | collective-permute-start | bytes 3145736 | tf_op jit(solution)/shard_map/ppermute | solution.py:27
  8.8 19.1 %collective-permute-start.2 = (bf16[528,256]{1,0:T(8,128)(2,1)}, bf16[528,256]{1,0:T(8,128)(2,1)}, u32[]{:S(2)}, u32[]{:S(2)}) collective-permute-start(bf16[528,256]{1,0:T(8,128)(2,1)} %get-tuple-element.78), channel_id=1, source_target_pairs={{0,1},{1,2},{2,3},{3,0},{4,5},{5,6},{6,7},{7,4},{8,9},{9,10},{10,1... | collective-permute-start | bytes 811016 | tf_op jit(solution)/shard_map/ppermute | solution.py:409
  10.2 20.9 %collective-permute-start.3 = (bf16[528,256]{1,0:T(8,128)(2,1)}, bf16[528,256]{1,0:T(8,128)(2,1)}, u32[]{:S(2)}, u32[]{:S(2)}) collective-permute-start(bf16[528,256]{1,0:T(8,128)(2,1)} %get-tuple-element.79), channel_id=1, source_target_pairs={{0,2},{1,3},{2,0},{3,1},{4,6},{5,7},{6,4},{7,5},{8,10},{9,11},{10,... | collective-permute-start | bytes 811016 | tf_op jit(solution)/shard_map/ppermute | solution.py:409
  12.5 18.6 %collective-permute-start.4 = (bf16[528,256]{1,0:T(8,128)(2,1)}, bf16[528,256]{1,0:T(8,128)(2,1)}, u32[]{:S(2)}, u32[]{:S(2)}) collective-permute-start(bf16[528,256]{1,0:T(8,128)(2,1)} %get-tuple-element.80), channel_id=1, source_target_pairs={{0,3},{1,0},{2,1},{3,2},{4,7},{5,4},{6,5},{7,6},{8,11},{9,8},{10,9... | collective-permute-start | bytes 811016 | tf_op jit(solution)/shard_map/ppermute | solution.py:409
  22.5 4.8 %copy-start = (s32[2048]{0:T(1024)S(1)}, s32[2048]{0:T(1024)}, u32[]{:S(2)}) copy-start(s32[2048]{0:T(1024)} %param.13) | copy-start | bytes 24580
  24.6 64.5 %collective-permute-start = (bf16[2,2,1024,128]{3,2,1,0:T(8,128)(2,1)}, bf16[2,2,1024,128]{3,2,1,0:T(8,128)(2,1)}, u32[]{:S(2)}, u32[]{:S(2)}) collective-permute-start(bf16[2,2,1024,128]{3,2,1,0:T(8,128)(2,1)} %rims.1), channel_id=1, source_target_pairs={{0,4},{4,8},{8,12},{12,16},{16,20},{20,24},{24,28},{1,5},{5,9},{9,... | collective-permute-start | bytes 3145736 | tf_op jit(solution)/shard_map/ppermute | solution.py:27
  31.0 25.5 %collective-permute-start.5 = (bf16[528,256]{1,0:T(8,128)(2,1)}, bf16[528,256]{1,0:T(8,128)(2,1)}, u32[]{:S(2)}, u32[]{:S(2)}) collective-permute-start(bf16[528,256]{1,0:T(8,128)(2,1)} %get-tuple-element.89), channel_id=1, source_target_pairs={{0,1},{1,2},{2,3},{3,0},{4,5},{5,6},{6,7},{7,4},{8,9},{9,10},{10,1... | collective-permute-start | bytes 811016 | tf_op jit(solution)/shard_map/ppermute | solution.py:409
  37.1 19.9 %collective-permute-start.6 = (bf16[528,256]{1,0:T(8,128)(2,1)}, bf16[528,256]{1,0:T(8,128)(2,1)}, u32[]{:S(2)}, u32[]{:S(2)}) collective-permute-start(bf16[528,256]{1,0:T(8,128)(2,1)} %get-tuple-element.90), channel_id=1, source_target_pairs={{0,2},{1,3},{2,0},{3,1},{4,6},{5,7},{6,4},{7,5},{8,10},{9,11},{10,... | collective-permute-start | bytes 811016 | tf_op jit(solution)/shard_map/ppermute | solution.py:409
  38.4 18.6 %collective-permute-start.7 = (bf16[528,256]{1,0:T(8,128)(2,1)}, bf16[528,256]{1,0:T(8,128)(2,1)}, u32[]{:S(2)}, u32[]{:S(2)}) collective-permute-start(bf16[528,256]{1,0:T(8,128)(2,1)} %get-tuple-element.91), channel_id=1, source_target_pairs={{0,3},{1,0},{2,1},{3,2},{4,7},{5,4},{6,5},{7,6},{8,11},{9,8},{10,9... | collective-permute-start | bytes 811016 | tf_op jit(solution)/shard_map/ppermute | solution.py:409
  57.0 28.8 %collective-permute-start.10 = (bf16[528,256]{1,0:T(8,128)(2,1)}, bf16[528,256]{1,0:T(8,128)(2,1)}, u32[]{:S(2)}, u32[]{:S(2)}) collective-permute-start(bf16[528,256]{1,0:T(8,128)(2,1)} %get-tuple-element.107), channel_id=1, source_target_pairs={{0,2},{1,3},{2,0},{3,1},{4,6},{5,7},{6,4},{7,5},{8,10},{9,11},{10,... | collective-permute-start | bytes 811016 | tf_op jit(solution)/shard_map/ppermute | solution.py:409
  62.0 23.7 %collective-permute-start.11 = (bf16[528,256]{1,0:T(8,128)(2,1)}, bf16[528,256]{1,0:T(8,128)(2,1)}, u32[]{:S(2)}, u32[]{:S(2)}) collective-permute-start(bf16[528,256]{1,0:T(8,128)(2,1)} %get-tuple-element.108), channel_id=1, source_target_pairs={{0,3},{1,0},{2,1},{3,2},{4,7},{5,4},{6,5},{7,6},{8,11},{9,8},{10,9... | collective-permute-start | bytes 811016 | tf_op jit(solution)/shard_map/ppermute | solution.py:409
  65.1 20.6 %collective-permute-start.9 = (bf16[528,256]{1,0:T(8,128)(2,1)}, bf16[528,256]{1,0:T(8,128)(2,1)}, u32[]{:S(2)}, u32[]{:S(2)}) collective-permute-start(bf16[528,256]{1,0:T(8,128)(2,1)} %get-tuple-element.106), channel_id=1, source_target_pairs={{0,1},{1,2},{2,3},{3,0},{4,5},{5,6},{6,7},{7,4},{8,9},{9,10},{10,1... | collective-permute-start | bytes 811016 | tf_op jit(solution)/shard_map/ppermute | solution.py:409
  82.5 27.0 %collective-permute-start.13 = (bf16[528,256]{1,0:T(8,128)(2,1)}, bf16[528,256]{1,0:T(8,128)(2,1)}, u32[]{:S(2)}, u32[]{:S(2)}) collective-permute-start(bf16[528,256]{1,0:T(8,128)(2,1)} %get-tuple-element.110), channel_id=1, source_target_pairs={{0,3},{1,0},{2,1},{3,2},{4,7},{5,4},{6,5},{7,6},{8,11},{9,8},{10,9... | collective-permute-start | bytes 811016 | tf_op jit(solution)/shard_map/ppermute | solution.py:409
  85.8 23.7 %collective-permute-start.8 = (bf16[528,256]{1,0:T(8,128)(2,1)}, bf16[528,256]{1,0:T(8,128)(2,1)}, u32[]{:S(2)}, u32[]{:S(2)}) collective-permute-start(bf16[528,256]{1,0:T(8,128)(2,1)} %get-tuple-element.104), channel_id=1, source_target_pairs={{0,1},{1,2},{2,3},{3,0},{4,5},{5,6},{6,7},{7,4},{8,9},{9,10},{10,1... | collective-permute-start | bytes 811016 | tf_op jit(solution)/shard_map/ppermute | solution.py:409
  85.8 23.7 %collective-permute-start.12 = (bf16[528,256]{1,0:T(8,128)(2,1)}, bf16[528,256]{1,0:T(8,128)(2,1)}, u32[]{:S(2)}, u32[]{:S(2)}) collective-permute-start(bf16[528,256]{1,0:T(8,128)(2,1)} %get-tuple-element.109), channel_id=1, source_target_pairs={{0,2},{1,3},{2,0},{3,1},{4,6},{5,7},{6,4},{7,5},{8,10},{9,11},{10,... | collective-permute-start | bytes 811016 | tf_op jit(solution)/shard_map/ppermute | solution.py:409
  106.5 27.7 %collective-permute-start.14 = (bf16[3,2,1024,128]{3,2,1,0:T(8,128)(2,1)}, bf16[3,2,1024,128]{3,2,1,0:T(8,128)(2,1)}, u32[]{:S(2)}, u32[]{:S(2)}) collective-permute-start(bf16[3,2,1024,128]{3,2,1,0:T(8,128)(2,1)} %get-tuple-element.131), channel_id=1, source_target_pairs={{4,0},{8,4},{12,8},{16,12},{20,16},{24,20},{28,24},{5,1},{9,5},{13... | collective-permute-start | bytes 4718600 | tf_op jit(solution)/shard_map/ppermute | solution.py:27
  119.3 14.8 %collective-permute-start.15 = (bf16[1,2,1024,128]{3,2,1,0:T(8,128)(2,1)}, bf16[1,2,1024,128]{3,2,1,0:T(8,128)(2,1)}, u32[]{:S(2)}, u32[]{:S(2)}) collective-permute-start(bf16[1,2,1024,128]{3,2,1,0:T(8,128)(2,1)} %get-tuple-element.132), channel_id=1, source_target_pairs={{4,0},{8,4},{12,8},{16,12},{20,16},{24,20},{28,24},{5,1},{9,5},{13... | collective-permute-start | bytes 1572872 | tf_op jit(solution)/shard_map/ppermute | solution.py:27
